TPU v7x, 32 devices: a whole 2x2x4 slice. The times are simulated.
32 devices in a mesh: grp: 2 (over y), tile: 4 (over z), row: 2 (over x), sub: 2 (over core).
Axes of the slice: x: 2, y: 2, z: 4, core: 2. Of those that a mesh axis runs over, the one named last changes fastest.
Arguments:
- velocity: float32 [2, 480, 960], P(None, ('grp', 'row'), ('tile', 'sub')), parts along dimension 1, may hold values from -10 to 10, as said below
- wet_bits: int32 [16, 960], P(('grp', 'row'), ('tile', 'sub')), parts along dimension 0, may hold values from 0 to 1073741823, as said below
- east_face: int32 [4], replicated, may hold values from 0 to 3, as said below
- seam_turn: int32 [4], replicated, may hold values from 0 to 3
Outputs:
- forcing: float32 [2, 120, 240], P(None, ('grp', 'row'), ('tile', 'sub')), parts along dimension 1
There are 2 independent parts, one for each index of `grp`. A program takes and returns all parts, laid end to end along the dimension named above; an argument that names none is the same for every part. Nothing has to cross between parts.
Inputs may be any that keep to these rules, and one draw needn't show every extreme that they name: `velocity`: gentle combinations of a few waves plus independent cell-to-cell parts. Bit b of wet_bits[j, x] is 1 where cell (30 j + b, x) is wet and 0 on land. `east_face`: each face is east of exactly one face.
All inputs are finite; a program needn't handle non-finite values.
Results may differ from a plain program's by a relative error of at most 0.000098.
Values sent between devices are 32-bit elements; how exact they have to be, the bound alone decides.
A program may use at most 64 MiB of HBM per device.

v0:
```python
import jax
import jax.numpy as jnp
from jax import lax
from jax.sharding import PartitionSpec as P

R = 32


deriv_scale = 8.0


def with_halo(value, sides, width, wrap):
    for axis, dim in sides:
        count, length = (lax.axis_size(axis), value.shape[dim])
        up = [(i, (i + 1) % count) for i in range(count if wrap else count - 1)]
        down = [(j, i) for i, j in up]
        last = lax.slice_in_dim(value, length - width, length, axis=dim)
        first = lax.slice_in_dim(value, 0, width, axis=dim)
        before = lax.ppermute(last, axis, up)
        after = lax.ppermute(first, axis, down)
        value = jnp.concatenate([before, value, after], axis=dim)
    return value


def unpack(wet_bits):
    repeated = jnp.repeat(wet_bits, 30, axis=0)
    shifts = lax.broadcasted_iota(jnp.int32, repeated.shape, 0) % 30
    return (jnp.right_shift(repeated, shifts) & 1).astype(jnp.float32)


def banded(n_in, n_out):
    offset = (
        jnp.arange(n_in, dtype=jnp.int32)[:, None] - jnp.arange(n_out, dtype=jnp.int32)[None, :]
    )
    spread = R * 1.0
    centred = (offset - R).astype(jnp.float32)
    taps = (jnp.arange(2 * R + 1, dtype=jnp.int32) - R).astype(jnp.float32)
    weight_sum = jnp.sum(jnp.exp(-0.5 * (taps / spread) ** 2))
    inside = (offset >= 0) & (offset <= 2 * R)
    return jnp.where(inside, jnp.exp(-0.5 * (centred / spread) ** 2) / weight_sum, jnp.float32(0.0))


def rotate(strip, turn):
    cosine = jnp.where(turn == 0, 1.0, jnp.where(turn == 2, -1.0, 0.0)).astype(jnp.float32)
    sine_part = jnp.where(turn == 1, 1.0, jnp.where(turn == 3, -1.0, 0.0)).astype(jnp.float32)
    return jnp.stack(
        [cosine * strip[0] - sine_part * strip[1], sine_part * strip[0] + cosine * strip[1]]
    )


def derive(padded):
    centre = padded[:, 1:-1, ..., 1:-1]
    grad_x = deriv_scale * (padded[:, 1:-1, ..., 2:] - padded[:, 1:-1, ..., :-2])
    grad_y = deriv_scale * (padded[:, 2:, ..., 1:-1] - padded[:, :-2, ..., 1:-1])
    advect = centre[0] * grad_x + centre[1] * grad_y
    return jnp.concatenate([centre, grad_x, grad_y, advect], axis=0)


def combine(smooth):
    east_part = smooth[6] - (smooth[0] * smooth[2] + smooth[1] * smooth[4])
    north_part = smooth[7] - (smooth[0] * smooth[3] + smooth[1] * smooth[5])
    return jnp.stack([east_part, north_part])


def pick(table, index):
    return lax.dynamic_index_in_dim(table, index, 0, keepdims=False)


def on_device(velocity, wet_bits, east_face, seam_turn):
    n_rows = velocity.shape[1]
    n_cols = velocity.shape[2]
    wet = unpack(wet_bits)
    field = velocity * wet[None]
    rim_width = R + 1
    row_count = lax.axis_size("row")
    tile_at = lax.axis_index("tile")
    sub_at = lax.axis_index("sub")
    row_at = lax.axis_index("row")
    face_count = east_face.shape[0]
    y_depth = R + 1
    extended = with_halo(field, (("row", 1),), R + 1, False)
    face_ids = jnp.arange(face_count, dtype=jnp.int32)
    west_face = jnp.sum(jnp.where(east_face == tile_at, face_ids, 0))
    east_next = pick(east_face, tile_at)
    east_turn = pick(seam_turn, tile_at)
    west_turn = (4 - pick(seam_turn, west_face)) % 4
    inner = with_halo(extended, (("sub", 2),), rim_width, True)
    west_rim = inner[:, :, :rim_width]
    east_rim = inner[:, :, n_cols + rim_width :]
    outer = jnp.where(sub_at == 0, west_rim, east_rim)
    gathered = lax.all_gather(outer[None], "tile", axis=0, tiled=True)
    seam_west = rotate(pick(gathered, west_face), west_turn)
    seam_east = rotate(pick(gathered, east_next), east_turn)
    from_west = jnp.where(sub_at == 0, seam_west, west_rim)
    from_east = jnp.where(sub_at == 1, seam_east, east_rim)
    padded = jnp.concatenate([from_west, extended, from_east], axis=2)
    channels = derive(padded)
    global_row = row_at * n_rows - R + jnp.arange(n_rows + 2 * R, dtype=jnp.int32)
    valid = ((global_row >= 0) & (global_row < row_count * n_rows)).astype(jnp.float32)
    channels = channels * valid[None, :, None]
    along = jnp.einsum(
        "cyx,xj->cyj", channels, banded(n_cols + 2 * R, n_cols), precision=lax.Precision.HIGHEST
    )
    smooth = jnp.einsum(
        "ki,ckx->cix", banded(n_rows + 2 * R, n_rows), along, precision=lax.Precision.HIGHEST
    )
    fine = combine(smooth) * wet[None]
    return fine.reshape(2, n_rows // 4, 4, n_cols // 4, 4).mean(axis=(2, 4))


def solution(mesh):
    placed = (
        P(None, ("grp", "row"), ("tile", "sub")),
        P(("grp", "row"), ("tile", "sub")),
        P(),
        P(),
    )
    return jax.shard_map(
        on_device,
        mesh=mesh,
        in_specs=placed,
        out_specs=P(None, ("grp", "row"), ("tile", "sub")),
        check_vma=False,
    )
```

profile of v0, /device:TPU:0, one launch (start us, length us, event | category | flops | bytes accessed | tf_op | source)
XLA Modules:
  0.0 54.4 jit_solution(6808391245389461637)
XLA Ops:
  0.0 0.7 %broadcast_in_dim.23 = s32[4,30,120]{2,1,0:T(8,128)S(1)} broadcast(s32[4,120]{1,0:T(4,128)} %param.5), dimensions={0,2} | broadcast | bytes 59520 | tf_op jit(solution)/shard_map/broadcast_in_dim | solution.py:26
  0.9 1.0 %copy.22 = f32[2,120,120]{1,2,0:T(8,128)S(1)} copy(f32[2,120,120]{2,1,0:T(8,128)} %param.4) | data formatting | bytes 230400 | tf_op args[0]
  2.1 4.9 %collective-permute-start = (f32[2,33,120]{1,2,0:T(8,128)S(1)}, f32[2,33,120]{1,2,0:T(8,128)S(1)}, u32[]{:S(2)}, u32[]{:S(2)}) collective-permute-start(f32[2,33,120]{1,2,0:T(8,128)S(1)} %get-tuple-element.19), channel_id=1, source_target_pairs={{0,2},{1,3},{4,6},{5,7},{8,10},{9,11},{12,14},{13,15},{16,18},{17,... | collective-permute-start | bytes 95048 | tf_op jit(solution)/shard_map/ppermute | solution.py:19
  6.9 1.3 %collective-permute-start.1 = (f32[2,33,120]{1,2,0:T(8,128)S(1)}, f32[2,33,120]{1,2,0:T(8,128)S(1)}, u32[]{:S(2)}, u32[]{:S(2)}) collective-permute-start(f32[2,33,120]{1,2,0:T(8,128)S(1)} %get-tuple-element.20), channel_id=1, source_target_pairs={{2,0},{3,1},{6,4},{7,5},{10,8},{11,9},{14,12},{15,13},{18,16},{19,... | collective-permute-start | bytes 95048 | tf_op jit(solution)/shard_map/ppermute | solution.py:20
  8.3 3.2 %reshape.215 = s32[30,4,30,4]{3,2,1,0:T(8,128)} reshape(s32[4,30,120]{2,1,0:T(8,128)S(1)} %broadcast_in_dim.23) | data formatting | bytes 115200 | tf_op jit(solution)/shard_map/reshape | solution.py:26
  11.5 1.8 %and_convert_fusion = f32[30,4,30,4]{3,2,1,0:T(8,128)S(1)} fusion(s32[30,4,30,4]{3,2,1,0:T(8,128)} %reshape.215, s32[30,4]{1,0:T(8,128)S(1)} %get-tuple-element.25, s32[30,4]{1,0:T(8,128)S(1)} %get-tuple-element.26, pred[30,4]{1,0:T(8,128)(4,1)S(1)} %compare_and_fusion), kind=kLoop, calls=%fused_computation | loop fusion | flops 57600 | bytes 116280 | tf_op jit(solution)/shard_map/convert_element_type | solution.py:28
  13.4 0.6 %fusion.23 = s32[]{:T(128)} fusion(s32[4]{0:T(128)S(1)} %copy-done.1, s32[]{:T(128)S(6)} %axis_index.35), kind=kLoop, calls=%fused_computation.59 | loop fusion | flops 11 | bytes 24 | tf_op jit(solution)/shard_map/reduce_sum | solution.py:83
  14.2 0.5 collective-permute-start.3
  14.7 0.7 %dynamic_slice.20 = s32[1]{0:T(128)} dynamic-slice(s32[4]{0:T(128)S(1)} %copy-done.1, s32[]{:T(128)S(6)} %select_n.106), dynamic_slice_sizes={1} | dynamic-slice | bytes 12 | tf_op jit(solution)/shard_map/jit(dynamic_index_in_dim)/dynamic_slice | solution.py:66
  18.7 0.6 %fusion.37 = (s32[1]{0:T(128)}, s32[1]{0:T(128)}) fusion(s32[4]{0:T(128)S(1)} %copy-done, s32[]{:T(128)S(6)} %select_n.96, s32[]{:T(128)S(6)} %select_n.106), kind=kLoop, calls=%fused_computation.76 | loop fusion | bytes 24 | tf_op jit(solution)/shard_map/jit(dynamic_index_in_dim)/dynamic_slice | solution.py:66
  22.2 0.8 %copy.28 = f32[30,4,30,4]{2,3,1,0:T(4,128)S(1)} copy(f32[30,4,30,4]{3,2,1,0:T(8,128)S(1)} %and_convert_fusion) | data formatting | bytes 115200 | tf_op jit(solution)/shard_map/convert_element_type | solution.py:28
  23.8 0.6 %exponential_reduce_fusion = f32[]{:T(128)} fusion(), kind=kLoop, calls=%fused_computation.60 | loop fusion | flops 389 | bytes 4 | tf_op jit(solution)/shard_map/reduce_sum | solution.py:38
  24.4 14.6 %all-gather = f32[8,186,33]{1,2,0:T(8,128)S(1)} all-gather(f32[2,186,33]{1,2,0:T(8,128)S(1)} %broadcast_select_fusion), channel_id=2, replica_groups=mesh['grp'=2,'tile'=4,'row'=2,'sub'=2] {'tile'}, dimensions={0}, use_global_device_ids=true | all-gather | bytes 245520 | tf_op jit(solution)/shard_map/all_gather | solution.py:91
  39.0 0.2 pad_maximum_fusion
  39.2 0.2 fusion.10
  39.4 0.5 fusion.35
  39.9 3.5 %fusion = f32[8,184,120]{2,1,0:T(8,128)S(1)} fusion(f32[2,184,184]{1,2,0:T(8,128)S(1)} %get-tuple-element.8, f32[2,184,184]{1,2,0:T(8,128)S(1)} %get-tuple-element.9, f32[2,184,184]{1,2,0:T(8,128)S(1)} %get-tuple-element.10, f32[2,184,184]{1,2,0:T(8,128)S(1)} %get-tuple-element.7, f32[184]{0:T(256)S(1)} %and_convert_fusion.2, f32[]{:T(128)} %exponential_reduce_fusion), kind=kOutput, calls=%fused_computation.2 | convolution fusion | flops 391347392 | bytes 1790692 | tf_op jit(solution)/shard_map/cyx,xj->cyj/dot_general | solution.py:101
  43.4 2.3 %convolution_bitcast_fusion = f32[8,120,120]{1,2,0:T(8,128)S(1)} fusion(f32[8,184,120]{2,1,0:T(8,128)S(1)} %fusion, f32[]{:T(128)} %exponential_reduce_fusion), kind=kOutput, calls=%fused_computation.9 | convolution fusion | flops 254604480 | bytes 1167364 | tf_op jit(solution)/shard_map/ki,ckx->cix/dot_general | solution.py:104
  45.8 1.9 %reshape.218 = f32[1,30,4,30,4]{2,1,4,3,0:T(8,128)S(1)} reshape(f32[1,120,120]{1,2,0:T(8,128)S(1)} %get-tuple-element.5) | data formatting | bytes 115200 | tf_op jit(solution)/shard_map/stack | solution.py:62
  47.7 1.9 %copy.26 = f32[1,30,4,30,4]{3,4,2,1,0:T(4,128)S(1)} copy(f32[1,30,4,30,4]{2,1,4,3,0:T(8,128)S(1)} %reshape.218) | data formatting | bytes 115200 | tf_op jit(solution)/shard_map/stack | solution.py:62
  49.6 1.9 %reshape.219 = f32[1,30,4,30,4]{2,1,4,3,0:T(8,128)S(1)} reshape(f32[1,120,120]{1,2,0:T(8,128)S(1)} %get-tuple-element.6) | data formatting | bytes 115200 | tf_op jit(solution)/shard_map/stack | solution.py:62
  51.5 1.9 %copy.27 = f32[1,30,4,30,4]{3,4,2,1,0:T(4,128)S(1)} copy(f32[1,30,4,30,4]{2,1,4,3,0:T(8,128)S(1)} %reshape.219) | data formatting | bytes 115200 | tf_op jit(solution)/shard_map/stack | solution.py:62
  53.5 0.3 fusion.8
  53.7 0.6 %copy.30 = f32[2,30,30]{2,0,1:T(2,128)} copy(f32[2,30,30]{2,1,0:T(8,128)S(1)} %broadcast_multiply_fusion.3) | data formatting | bytes 14400 | tf_op jit(solution)/shard_map/div | solution.py:108
  (26 shorter events, 0.7 us)
Async XLA Ops:
  2.1 11.9 %collective-permute-start = (f32[2,33,120]{1,2,0:T(8,128)S(1)}, f32[2,33,120]{1,2,0:T(8,128)S(1)}, u32[]{:S(2)}, u32[]{:S(2)}) collective-permute-start(f32[2,33,120]{1,2,0:T(8,128)S(1)} %get-tuple-element.19), channel_id=1, source_target_pairs={{0,2},{1,3},{4,6},{5,7},{8,10},{9,11},{12,14},{13,15},{16,18},{17,... | collective-permute-start | bytes 95048 | tf_op jit(solution)/shard_map/ppermute | solution.py:19
  6.9 7.1 %collective-permute-start.1 = (f32[2,33,120]{1,2,0:T(8,128)S(1)}, f32[2,33,120]{1,2,0:T(8,128)S(1)}, u32[]{:S(2)}, u32[]{:S(2)}) collective-permute-start(f32[2,33,120]{1,2,0:T(8,128)S(1)} %get-tuple-element.20), channel_id=1, source_target_pairs={{2,0},{3,1},{6,4},{7,5},{10,8},{11,9},{14,12},{15,13},{18,16},{19,... | collective-permute-start | bytes 95048 | tf_op jit(solution)/shard_map/ppermute | solution.py:20
  11.5 1.9 %copy-start.1 = (s32[4]{0:T(128)S(1)}, s32[4]{0:T(128)}, u32[]{:S(2)}) copy-start(s32[4]{0:T(128)} %param.6) | copy-start | bytes 52
  11.5 7.2 %copy-start = (s32[4]{0:T(128)S(1)}, s32[4]{0:T(128)}, u32[]{:S(2)}) copy-start(s32[4]{0:T(128)} %param.7) | copy-start | bytes 52
  14.1 10.3 %collective-permute-start.2 = (f32[2,186,33]{1,2,0:T(8,128)S(1)}, f32[2,186,33]{1,2,0:T(8,128)S(1)}, u32[]{:S(2)}, u32[]{:S(2)}) collective-permute-start(f32[2,186,33]{1,2,0:T(8,128)S(1)} %get-tuple-element.13), channel_id=1, source_target_pairs={{0,1},{1,0},{2,3},{3,2},{4,5},{5,4},{6,7},{7,6},{8,9},{9,8},{10,11... | collective-permute-start | bytes 147320 | tf_op jit(solution)/shard_map/ppermute | solution.py:19
  14.2 10.2 %collective-permute-start.3 = (f32[2,186,33]{1,2,0:T(8,128)S(1)}, f32[2,186,33]{1,2,0:T(8,128)S(1)}, u32[]{:S(2)}, u32[]{:S(2)}) collective-permute-start(f32[2,186,33]{1,2,0:T(8,128)S(1)} %get-tuple-element.14), channel_id=1, source_target_pairs={{1,0},{0,1},{3,2},{2,3},{5,4},{4,5},{7,6},{6,7},{9,8},{8,9},{11,10... | collective-permute-start | bytes 147320 | tf_op jit(solution)/shard_map/ppermute | solution.py:20
where the time goes:
time: 55 us; the launch traced here: 54.4 us
  local copies, waits for them, and re-layouts  15.5 us (28%)
  blocking collectives  14.6 us (27%)
  between operations  7.18 us (13%)
  starting transfers between devices  6.72 us (12%)
  matrix products  5.89 us (11%)
  other arithmetic  4.56 us (8%)
    all_gather x1, blocking collectives, on_device(): gathered = lax.all_gather(outer[None], 'tile', axis=0, tiled=True)  14.6 us
    another operation x4, local copies, waits for them, and re-layouts, combine(): return jnp.stack([east_part, north_part])  7.64 us
    ppermute x2, starting transfers between devices, with_halo(): before = lax.ppermute(last, axis, up)  4.93 us
    dot_general x1, matrix products, on_device(): jnp.einsum('cyx,xj->cyj', channels, banded(n_cols + 2 * R, n_cols), preci...  3.54 us
    reshape x2, local copies, waits for them, and re-layouts, unpack(): repeated = jnp.repeat(wet_bits, 30, axis=0)  3.24 us
    dot_general x1, matrix products, on_device(): jnp.einsum('ki,ckx->cix', banded(n_rows + 2 * R, n_rows), along, precisio...  2.34 us
    convert_element_type x2, other arithmetic, unpack(): return (jnp.right_shift(repeated, shifts) & 1).astype(jnp.float32)  1.95 us
    ppermute x2, starting transfers between devices, with_halo(): after = lax.ppermute(first, axis, down)  1.79 us
  transfers between devices with their start and end apart: 4, of which 0 were waited for; matrix products, arithmetic and copies ran while one was open for 16% of the time, Pallas kernels for 0%

commit v1 on v0

v1 whole, which is shorter than its diff:
```python
import functools
import math

import jax
import jax.numpy as jnp
from jax import lax
from jax.experimental import pallas as pl
from jax.experimental.pallas import tpu as pltpu
from jax.sharding import PartitionSpec as P

R = 32
RIM = R + 1
LANES = 128
RING = 2 * LANES
DERIV_SCALE = 8.0
POOL = 4
WORD_ROWS = 30
MESH = pl.DeviceIdType.MESH

WEIGHT_SUM = sum(math.exp(-0.5 * (k / R) ** 2) for k in range(-R, R + 1))


def ceil_to(value, step):
    return -(-value // step) * step


def gaussian(distance, keep):
    d = distance.astype(jnp.float32) * (1.0 / R)
    weight = jnp.exp(-0.5 * d * d) * (1.0 / WEIGHT_SUM)
    return jnp.where(keep & (jnp.abs(distance) <= R), weight, 0.0)


def split(value):
    high = value.astype(jnp.bfloat16)
    low = (value - high.astype(jnp.float32)).astype(jnp.bfloat16)
    return high, low


def dot(a, b):
    return jnp.dot(a, b, preferred_element_type=jnp.float32)


def roll(value, shift, axis=1):
    size = value.shape[axis]
    shift = shift % size
    return value if shift == 0 else pltpu.roll(value, shift, axis)


def kernel(
    face_ref, turn_ref, vel_hbm, bits_hbm, out_ref,
    vel, bits, ext, strips, seams, ring, pooled,
    load_sem, row_send, row_recv, strip_send, strip_recv,
):
    tiles, rows = lax.axis_size("tile"), lax.axis_size("row")
    grp, tile, row, sub = (lax.axis_index(a) for a in ("grp", "tile", "row", "sub"))
    n_rows, n_cols = vel.shape[1], vel.shape[2]
    halo = ceil_to(RIM, 8)
    has_up, has_down = row > 0, row < rows - 1
    other = 1 - sub

    loads = [
        pltpu.make_async_copy(vel_hbm, vel, load_sem.at[0]),
        pltpu.make_async_copy(bits_hbm, bits, load_sem.at[1]),
    ]
    for load in loads:
        load.start()

    barrier = pltpu.get_barrier_semaphore()

    def greet(t, r, s):
        pl.semaphore_signal(barrier, inc=1, device_id=(grp, t, r, s), device_id_type=MESH)

    for k in range(tiles):
        t = lax.rem(tile + k, tiles)
        greet(t, row, other)

        @pl.when(has_up)
        def _():
            greet(t, row - 1, other)

        @pl.when(has_down)
        def _():
            greet(t, row + 1, other)

    @pl.when(has_up)
    def _():
        greet(tile, row - 1, sub)

    @pl.when(has_down)
    def _():
        greet(tile, row + 1, sub)

    for load in loads:
        load.wait()

    row_id = lax.broadcasted_iota(jnp.int32, (n_rows, n_cols), 0)
    words = bits[...]
    word = jnp.broadcast_to(words[0:1], (n_rows, n_cols))
    bit = row_id
    for j in range(1, words.shape[0]):
        here = row_id >= j * WORD_ROWS
        word = jnp.where(here, words[j : j + 1], word)
        bit = jnp.where(here, row_id - j * WORD_ROWS, bit)
    wet = (jnp.right_shift(word, bit) & 1).astype(jnp.float32)
    for c in range(2):
        ext[c, halo : halo + n_rows, 0:n_cols] = vel[c] * wet

    lane = lax.broadcasted_iota(jnp.int32, (halo, LANES), 1)

    def pack(start):
        def block(c, g, place):
            rows_at = halo + g * halo
            return roll(ext[c, rows_at : rows_at + halo, :], place * RIM - start)

        def join(a, b, c):
            rest = jnp.where(lane < 3 * RIM, c, 0.0)
            return jnp.where(lane < RIM, a, jnp.where(lane < 2 * RIM, b, rest))

        first = join(block(0, 0, 0), block(1, 0, 1), block(0, 1, 2))
        last = join(block(0, 2, 0), block(1, 2, 1), block(1, 1, 2))
        return first, last

    west_cols, east_cols = pack(0), pack(n_cols - RIM)
    at_west = sub == 0
    for i in range(2):
        at = slice(i * halo, (i + 1) * halo)
        strips[0, at, :] = jnp.where(at_west, west_cols[i], east_cols[i])
        strips[1, at, :] = jnp.where(at_west, east_cols[i], west_cols[i])

    @pl.when(jnp.logical_not(has_up))
    def _():
        ext[:, 0:halo, :] = jnp.zeros((2, halo, LANES), jnp.float32)
        seams[:, 0:halo, :] = jnp.zeros((tiles + 1, halo, LANES), jnp.float32)

    @pl.when(jnp.logical_not(has_down))
    def _():
        ext[:, halo + n_rows :, :] = jnp.zeros((2, halo, LANES), jnp.float32)
        seams[:, 3 * halo :, :] = jnp.zeros((tiles + 1, halo, LANES), jnp.float32)

    n_beside = has_up.astype(jnp.int32) + has_down.astype(jnp.int32)
    pl.semaphore_wait(barrier, tiles + n_beside * (tiles + 1))

    def strip_copy(which, slot, part, k, t, r):
        source = ((0, 2 * halo), (halo, halo), (0, halo))[part]
        target = (halo, 0, 3 * halo)[part]
        return pltpu.make_async_remote_copy(
            src_ref=strips.at[which, pl.ds(*source)],
            dst_ref=seams.at[slot, pl.ds(target, source[1])],
            send_sem=strip_send.at[part, k],
            recv_sem=strip_recv.at[part, slot],
            device_id=(grp, t, r, other),
            device_id_type=MESH,
        )

    def row_copy(part, r):
        source = (halo + n_rows - halo, halo)[part - 1]
        target = (0, halo + n_rows)[part - 1]
        return pltpu.make_async_remote_copy(
            src_ref=ext.at[:, pl.ds(source, halo)],
            dst_ref=ext.at[:, pl.ds(target, halo)],
            send_sem=row_send.at[part - 1],
            recv_sem=row_recv.at[part - 1],
            device_id=(grp, tile, r, sub),
            device_id_type=MESH,
        )

    def sends(act, part, r):
        for k in reversed(range(tiles)):
            act(strip_copy(0, tile, part, k, lax.rem(tile + k, tiles), r))
        act(strip_copy(1, tiles, part, tiles, tile, r))
        if part:
            act(row_copy(part, r))

    def all_sends(act):
        sends(act, 0, row)

        @pl.when(has_down)
        def _():
            sends(act, 1, row + 1)

        @pl.when(has_up)
        def _():
            sends(act, 2, row - 1)

    all_sends(lambda copy: copy.start())

    place = lax.broadcasted_iota(jnp.int32, (RING, LANES), 0)
    x_out = lax.broadcasted_iota(jnp.int32, (RING, LANES), 1)
    x_in = jnp.where(place < (n_cols + RING) // 2, place, place - RING)
    x_high, x_low = split(gaussian(x_in - x_out, x_out < n_cols))
    top = halo - R
    span = ceil_to(n_rows + 2 * R, 16)
    span_out = ceil_to(n_rows, 16)
    y_out = lax.broadcasted_iota(jnp.int32, (span_out, span), 0)
    y_in = lax.broadcasted_iota(jnp.int32, (span_out, span), 1) - R
    y_global = y_in + row * n_rows
    inside = (y_global >= 0) & (y_global < rows * n_rows) & (y_out < n_rows)
    y_high, y_low = split(gaussian(y_in - y_out, inside))

    west = jnp.int32(0)
    for i in range(tiles):
        west = jnp.where(face_ref[i] == tile, i, west)
    east_turn = turn_ref[tile]
    west_turn = turn_ref[west]
    west_turn = jnp.where(west_turn == 0, 0, 4 - west_turn)
    beside = jnp.where(at_west, west, face_ref[tile])
    turn = jnp.where(at_west, west_turn, east_turn)

    def choose(a, b):
        return jnp.where(turn == a, 1.0, jnp.where(turn == b, -1.0, 0.0)).astype(jnp.float32)

    cosine, sine = choose(0, 2), choose(1, 3)

    def arrived(part):
        for slot in range(tiles + 1):
            strip_copy(0, slot, part, 0, tile, row).wait_recv()
        if part:
            row_copy(part, row).wait_recv()

    arrived(0)

    @pl.when(has_up)
    def _():
        arrived(1)

    @pl.when(has_down)
    def _():
        arrived(2)

    def unpack(packed, shift):
        a, b, c, d = (packed[i * halo : (i + 1) * halo] for i in range(4))
        places = (((a, 0), (b, 0), (b, 2), (c, 0), (d, 0)), ((a, 1), (b, 1), (c, 2), (c, 1), (d, 1)))
        return [
            jnp.concatenate([roll(v, shift - p * RIM) for v, p in blocks], axis=0) for blocks in places
        ]

    seam, inner = seams[beside], seams[tiles]
    east_u, east_v = unpack(jnp.where(at_west, inner, seam), n_cols)
    west_u, west_v = unpack(jnp.where(at_west, seam, inner), LANES - RIM)
    east_c = jnp.where(at_west, 1.0, cosine).astype(jnp.float32)
    east_s = jnp.where(at_west, 0.0, sine).astype(jnp.float32)
    west_c = jnp.where(at_west, cosine, 1.0).astype(jnp.float32)
    west_s = jnp.where(at_west, sine, 0.0).astype(jnp.float32)
    east_uv = (east_c * east_u - east_s * east_v, east_s * east_u + east_c * east_v)
    west_uv = (west_c * west_u - west_s * west_v, west_s * west_u + west_c * west_v)

    n_ext = ext.shape[1]
    lane = lax.broadcasted_iota(jnp.int32, (n_ext, LANES), 1)
    for c in range(2):
        ring[c, 0:n_ext, 0:LANES] = jnp.where(lane < n_cols, ext[c], east_uv[c])
        rest = jnp.where(lane >= LANES - RIM, west_uv[c], 0.0)
        ring[c, 0:n_ext, LANES:] = jnp.where(lane < n_cols + RIM - LANES, east_uv[c], rest)
        ring[c, n_ext:, :] = jnp.zeros((ring.shape[1] - n_ext, RING), jnp.float32)

    def derive(c):
        centre = ring[c, top : top + span, :]
        grad_x = DERIV_SCALE * (roll(centre, -1) - roll(centre, 1))
        grad_y = DERIV_SCALE * (ring[c, top + 1 : top + 1 + span, :] - ring[c, top - 1 : top - 1 + span, :])
        return centre, grad_x, grad_y

    u, u_x, u_y = derive(0)
    v, v_x, v_y = derive(1)
    channels = (u, v, u_x, v_x, u_y, v_y, u * u_x + v * u_y, u * v_x + v * v_y)

    def smoothed(first, second):
        along = []
        for channel in (first, second):
            high, low = split(channel)
            along.append(dot(high, x_high) + (dot(low, x_high) + dot(high, x_low)))
        high, low = split(jnp.concatenate(along, axis=1))
        both = dot(y_high, high) + (dot(y_high, low) + dot(y_low, high))
        return both[:n_rows, :n_cols], both[:n_rows, LANES : LANES + n_cols]

    smooth = []
    for i in range(0, 8, 2):
        smooth += smoothed(channels[i], channels[i + 1])
    fine = (
        smooth[6] - (smooth[0] * smooth[2] + smooth[1] * smooth[4]),
        smooth[7] - (smooth[0] * smooth[3] + smooth[1] * smooth[5]),
    )

    n_out = n_rows // POOL
    m_out = n_cols // POOL
    col = lax.broadcasted_iota(jnp.int32, (LANES, m_out), 0)
    block_at = lax.broadcasted_iota(jnp.int32, (LANES, m_out), 1) * POOL
    mean = jnp.where((col >= block_at) & (col < block_at + POOL), 1.0 / POOL**2, 0.0)
    mean = mean.astype(jnp.bfloat16)
    for c in range(2):
        pooled[c] = jnp.zeros((n_rows, LANES), jnp.float32)
        pooled[c, :, 0:n_cols] = fine[c] * wet
        total = pooled[c, pl.ds(0, n_out, stride=POOL), :]
        for k in range(1, POOL):
            total = total + pooled[c, pl.ds(k, n_out, stride=POOL), :]
        high, low = split(total)
        out_ref[c] = dot(high, mean) + dot(low, mean)

    all_sends(lambda copy: copy.wait_send())


def on_device(velocity, wet_bits, east_face, seam_turn):
    _, n_rows, n_cols = velocity.shape
    tiles = lax.axis_size("tile")
    halo = ceil_to(RIM, 8)
    assert n_rows == 3 * halo and lax.axis_size("sub") == 2
    assert RIM <= n_cols <= LANES and n_cols + 2 * RIM <= RING and 3 * RIM <= LANES
    n_ext = n_rows + 2 * halo
    f32 = jnp.float32
    return pl.pallas_call(
        kernel,
        out_shape=jax.ShapeDtypeStruct((2, n_rows // POOL, n_cols // POOL), f32),
        in_specs=[
            pl.BlockSpec(memory_space=pltpu.SMEM),
            pl.BlockSpec(memory_space=pltpu.SMEM),
            pl.BlockSpec(memory_space=pl.ANY),
            pl.BlockSpec(memory_space=pl.ANY),
        ],
        out_specs=pl.BlockSpec(memory_space=pltpu.VMEM),
        scratch_shapes=[
            pltpu.VMEM(velocity.shape, f32),
            pltpu.VMEM(wet_bits.shape, jnp.int32),
            pltpu.VMEM((2, n_ext, LANES), f32),
            pltpu.VMEM((2, 2 * halo, LANES), f32),
            pltpu.VMEM((tiles + 1, 4 * halo, LANES), f32),
            pltpu.VMEM((2, n_ext + 8, RING), f32),
            pltpu.VMEM((2, n_rows, LANES), f32),
            pltpu.SemaphoreType.DMA((2,)),
            pltpu.SemaphoreType.DMA((2,)),
            pltpu.SemaphoreType.DMA((2,)),
            pltpu.SemaphoreType.DMA((3, tiles + 1)),
            pltpu.SemaphoreType.DMA((3, tiles + 1)),
        ],
        compiler_params=pltpu.CompilerParams(
            collective_id=0, has_side_effects=True, vmem_limit_bytes=32 * 1024 * 1024
        ),
    )(east_face, seam_turn, velocity, wet_bits)


def solution(mesh):
    placed = (
        P(None, ("grp", "row"), ("tile", "sub")),
        P(("grp", "row"), ("tile", "sub")),
        P(),
        P(),
    )
    return jax.shard_map(
        on_device,
        mesh=mesh,
        in_specs=placed,
        out_specs=P(None, ("grp", "row"), ("tile", "sub")),
        check_vma=False,
    )
```

time: 55 us -> 19.4 us (0.35)
  Pallas kernels: 0 us -> 15.7 us
  blocking collectives: 14.6 us -> 0 us
  local copies, waits for them, and re-layouts: 15.5 us -> 3.53 us
  between operations: 7.18 us -> 0.01 us
  starting transfers between devices: 6.72 us -> 0 us
  matrix products: 5.89 us -> 0 us
  other arithmetic: 4.56 us -> 0 us
    pallas_call x0 -> x1, Pallas kernels: none -> 15.7 us  [on_device(): pl.pallas_call(kernel, out_shape=jax.ShapeDtypeStruct((2, n_rows // POOL,...]
    all_gather x1 -> x0, blocking collectives: 14.6 us -> none  [on_device(): gathered = lax.all_gather(outer[None], 'tile', axis=0, tiled=True)]
    another operation x4 -> x0, local copies, waits for them, and re-layouts: 7.64 us -> none  [combine(): return jnp.stack([east_part, north_part])]
    ppermute x4 -> x0, starting transfers between devices: 6.72 us -> none  [the longest x2 4.93 us: with_halo(): before = lax.ppermute(last, axis, up)]
    dot_general x2 -> x0, matrix products: 5.89 us -> none  [the longest x1 3.54 us: on_device(): jnp.einsum('cyx,xj->cyj', channels, banded(n_cols + 2 * R, n_cols), preci...]
    reshape x2 -> x0, local copies, waits for them, and re-layouts: 3.24 us -> none  [unpack(): repeated = jnp.repeat(wet_bits, 30, axis=0)]
    convert_element_type x3 -> x0, other arithmetic: 1.96 us -> none  [the longest x2 1.95 us: unpack(): return (jnp.right_shift(repeated, shifts) & 1).astype(jnp.float32)]
    unnamed x5 -> x8, local copies, waits for them, and re-layouts: 1 us -> 2.89 us
  transfers between devices with their start and end apart: 4 -> 0, of which waited for: 0 -> 0; matrix products, arithmetic and copies ran while one was open for 16% -> 0% of each run, Pallas kernels for 0% -> 0%
where the time goes in v1:
time: 19.4 us; the launch traced here: 19.3 us
  Pallas kernels  15.7 us (81%)
  local copies, waits for them, and re-layouts  3.53 us (18%)
    pallas_call x1, Pallas kernels, on_device(): pl.pallas_call(kernel, out_shape=jax.ShapeDtypeStruct((2, n_rows // POOL,...  15.7 us
    unnamed x8, local copies, waits for them, and re-layouts  2.89 us
    pallas_call x1, local copies, waits for them, and re-layouts, on_device(): pl.pallas_call(kernel, out_shape=jax.ShapeDtypeStruct((2, n_rows // POOL,...  0.64 us

profile of v1, /device:TPU:0, one launch (start us, length us, event | category | flops | bytes accessed | tf_op | source)
XLA Modules:
  0.0 19.3 jit_solution(8708366612513126805)
XLA Ops:
  0.0 0.0 copy-start
  0.0 0.9 %copy-done = f32[2,120,120]{2,1,0:T(8,128)S(1)} copy-done((f32[2,120,120]{2,1,0:T(8,128)S(1)}, f32[2,120,120]{2,1,0:T(8,128)}, u32[]{:S(2)}) %copy-start) | copy-done | bytes 115224
  0.9 0.0 copy-start.1
  0.9 0.7 %copy-done.1 = s32[4,120]{1,0:T(4,128)S(1)} copy-done((s32[4,120]{1,0:T(4,128)S(1)}, s32[4,120]{1,0:T(4,128)}, u32[]{:S(2)}) %copy-start.1) | copy-done | bytes 1944
  1.6 0.0 copy-start.2
  1.6 0.7 %copy-done.2 = s32[4]{0:T(128)S(1)} copy-done((s32[4]{0:T(128)S(1)}, s32[4]{0:T(128)}, u32[]{:S(2)}) %copy-start.2) | copy-done | bytes 40
  2.2 0.0 copy-start.3
  2.2 0.7 %copy-done.3 = s32[4]{0:T(128)S(1)} copy-done((s32[4]{0:T(128)S(1)}, s32[4]{0:T(128)}, u32[]{:S(2)}) %copy-start.3) | copy-done | bytes 40
  2.9 15.7 %shard_map.46 = f32[2,30,30]{2,1,0:T(8,128)S(1)} custom-call(s32[4]{0:T(128)S(1)} %copy-done.2, s32[4]{0:T(128)S(1)} %copy-done.3, f32[2,120,120]{2,1,0:T(8,128)S(1)} %copy-done, s32[4,120]{1,0:T(4,128)S(1)} %copy-done.1), custom_call_target="tpu_custom_call" | custom-call | tf_op jit(solution)/shard_map/pallas_call | solution.py:308
  18.6 0.6 %copy.5 = f32[2,30,30]{2,0,1:T(2,128)} copy(f32[2,30,30]{2,1,0:T(8,128)S(1)} %shard_map.46) | data formatting | bytes 14400 | tf_op jit(solution)/shard_map/pallas_call | solution.py:308
Async XLA Ops:
  0.0 0.9 %copy-start = (f32[2,120,120]{2,1,0:T(8,128)S(1)}, f32[2,120,120]{2,1,0:T(8,128)}, u32[]{:S(2)}) copy-start(f32[2,120,120]{2,1,0:T(8,128)} %vel_hbm.1) | copy-start | bytes 345604
  0.9 0.7 %copy-start.1 = (s32[4,120]{1,0:T(4,128)S(1)}, s32[4,120]{1,0:T(4,128)}, u32[]{:S(2)}) copy-start(s32[4,120]{1,0:T(4,128)} %bits_hbm.1) | copy-start | bytes 5764
  1.6 0.7 %copy-start.2 = (s32[4]{0:T(128)S(1)}, s32[4]{0:T(128)}, u32[]{:S(2)}) copy-start(s32[4]{0:T(128)} %face_ref.1) | copy-start | bytes 52
  2.2 0.7 %copy-start.3 = (s32[4]{0:T(128)S(1)}, s32[4]{0:T(128)}, u32[]{:S(2)}) copy-start(s32[4]{0:T(128)} %turn_ref.1) | copy-start | bytes 52

commit v2 on v1

--- a/solution.py
+++ b/solution.py
@@ -11,7 +11,7 @@
 R = 32
 RIM = R + 1
 LANES = 128
-RING = 2 * LANES
+EDGE = 2
 DERIV_SCALE = 8.0
 POOL = 4
 WORD_ROWS = 30
@@ -47,8 +47,8 @@
 
 
 def kernel(
-    face_ref, turn_ref, vel_hbm, bits_hbm, out_ref,
-    vel, bits, ext, strips, seams, ring, pooled,
+    face_hbm, turn_hbm, vel_hbm, bits_hbm, out_ref,
+    face_ref, turn_ref, vel, bits, ext, strips, seams, ring, inner_sum, pooled,
     load_sem, row_send, row_recv, strip_send, strip_recv,
 ):
     tiles, rows = lax.axis_size("tile"), lax.axis_size("row")
@@ -61,6 +61,8 @@
     loads = [
         pltpu.make_async_copy(vel_hbm, vel, load_sem.at[0]),
         pltpu.make_async_copy(bits_hbm, bits, load_sem.at[1]),
+        pltpu.make_async_copy(face_hbm, face_ref, load_sem.at[2]),
+        pltpu.make_async_copy(turn_hbm, turn_ref, load_sem.at[3]),
     ]
     for load in loads:
         load.start()
@@ -103,7 +105,9 @@
         bit = jnp.where(here, row_id - j * WORD_ROWS, bit)
     wet = (jnp.right_shift(word, bit) & 1).astype(jnp.float32)
     for c in range(2):
+        ext[c, halo : halo + n_rows, :] = jnp.zeros((n_rows, LANES), jnp.float32)
         ext[c, halo : halo + n_rows, 0:n_cols] = vel[c] * wet
+        ext[c, n_rows + 2 * halo :, :] = jnp.zeros((8, LANES), jnp.float32)
 
     lane = lax.broadcasted_iota(jnp.int32, (halo, LANES), 1)
 
@@ -134,7 +138,7 @@
 
     @pl.when(jnp.logical_not(has_down))
     def _():
-        ext[:, halo + n_rows :, :] = jnp.zeros((2, halo, LANES), jnp.float32)
+        ext[:, halo + n_rows : n_rows + 2 * halo, :] = jnp.zeros((2, halo, LANES), jnp.float32)
         seams[:, 3 * halo :, :] = jnp.zeros((tiles + 1, halo, LANES), jnp.float32)
 
     n_beside = has_up.astype(jnp.int32) + has_down.astype(jnp.int32)
@@ -184,10 +188,22 @@
 
     all_sends(lambda copy: copy.start())
 
-    place = lax.broadcasted_iota(jnp.int32, (RING, LANES), 0)
-    x_out = lax.broadcasted_iota(jnp.int32, (RING, LANES), 1)
-    x_in = jnp.where(place < (n_cols + RING) // 2, place, place - RING)
-    x_high, x_low = split(gaussian(x_in - x_out, x_out < n_cols))
+    west_lane = LANES - EDGE - RIM
+    place = lax.broadcasted_iota(jnp.int32, (LANES, LANES), 0)
+    x_out = lax.broadcasted_iota(jnp.int32, (LANES, LANES), 1)
+
+    def x_weights(x_in, keep):
+        high, low = split(gaussian(x_in - x_out, keep & (x_out < n_cols)))
+        above = jnp.concatenate([high, low], axis=1)
+        below = jnp.concatenate([high, jnp.zeros_like(low)], axis=1)
+        return jnp.concatenate([above, below], axis=0)
+
+    x_own = x_weights(place, (place >= 1) & (place <= n_cols - 2))
+    at_east = place < LANES // 2
+    x_edge = x_weights(
+        jnp.where(at_east, place + (n_cols - EDGE), place - (west_lane + RIM)),
+        ((place >= 1) & (place <= RIM)) | ((place > west_lane) & (place <= west_lane + RIM)),
+    )
     top = halo - R
     span = ceil_to(n_rows + 2 * R, 16)
     span_out = ceil_to(n_rows, 16)
@@ -214,8 +230,40 @@
     def arrived(part):
         for slot in range(tiles + 1):
             strip_copy(0, slot, part, 0, tile, row).wait_recv()
-        if part:
-            row_copy(part, row).wait_recv()
+
+    def derive(field, c):
+        centre = field[c, top : top + span, :]
+        grad_x = DERIV_SCALE * (roll(centre, -1) - roll(centre, 1))
+        grad_y = DERIV_SCALE * (field[c, top + 1 : top + 1 + span, :] - field[c, top - 1 : top - 1 + span, :])
+        return centre, grad_x, grad_y
+
+    def derived(field):
+        u, u_x, u_y = derive(field, 0)
+        v, v_x, v_y = derive(field, 1)
+        return u, v, u_x, v_x, u_y, v_y, u * u_x + v * u_y, u * v_x + v * v_y
+
+    def along(channel, weights):
+        both = dot(jnp.concatenate(split(channel), axis=1), weights)
+        return both[:, :LANES] + both[:, LANES:]
+
+    @pl.when(has_up)
+    def _():
+        row_copy(1, row).wait_recv()
+
+    @pl.when(has_down)
+    def _():
+        row_copy(2, row).wait_recv()
+
+    for i, channel in enumerate(derived(ext)):
+        inner_sum[i] = along(channel, x_own)
+
+    n_ext = n_rows + 2 * halo
+    lane = lax.broadcasted_iota(jnp.int32, (n_ext, LANES), 1)
+    for c in range(2):
+        own = ext[c, 0:n_ext, :]
+        rest = jnp.where(lane >= LANES - EDGE, roll(own, -EDGE), 0.0)
+        ring[c, 0:n_ext, :] = jnp.where(lane < EDGE, roll(own, EDGE - n_cols), rest)
+        ring[c, n_ext:, :] = jnp.zeros((8, LANES), jnp.float32)
 
     arrived(0)
 
@@ -235,8 +283,8 @@
         ]
 
     seam, inner = seams[beside], seams[tiles]
-    east_u, east_v = unpack(jnp.where(at_west, inner, seam), n_cols)
-    west_u, west_v = unpack(jnp.where(at_west, seam, inner), LANES - RIM)
+    east_u, east_v = unpack(jnp.where(at_west, inner, seam), EDGE)
+    west_u, west_v = unpack(jnp.where(at_west, seam, inner), west_lane)
     east_c = jnp.where(at_west, 1.0, cosine).astype(jnp.float32)
     east_s = jnp.where(at_west, 0.0, sine).astype(jnp.float32)
     west_c = jnp.where(at_west, cosine, 1.0).astype(jnp.float32)
@@ -244,36 +292,21 @@
     east_uv = (east_c * east_u - east_s * east_v, east_s * east_u + east_c * east_v)
     west_uv = (west_c * west_u - west_s * west_v, west_s * west_u + west_c * west_v)
 
-    n_ext = ext.shape[1]
-    lane = lax.broadcasted_iota(jnp.int32, (n_ext, LANES), 1)
     for c in range(2):
-        ring[c, 0:n_ext, 0:LANES] = jnp.where(lane < n_cols, ext[c], east_uv[c])
-        rest = jnp.where(lane >= LANES - RIM, west_uv[c], 0.0)
-        ring[c, 0:n_ext, LANES:] = jnp.where(lane < n_cols + RIM - LANES, east_uv[c], rest)
-        ring[c, n_ext:, :] = jnp.zeros((ring.shape[1] - n_ext, RING), jnp.float32)
-
-    def derive(c):
-        centre = ring[c, top : top + span, :]
-        grad_x = DERIV_SCALE * (roll(centre, -1) - roll(centre, 1))
-        grad_y = DERIV_SCALE * (ring[c, top + 1 : top + 1 + span, :] - ring[c, top - 1 : top - 1 + span, :])
-        return centre, grad_x, grad_y
-
-    u, u_x, u_y = derive(0)
-    v, v_x, v_y = derive(1)
-    channels = (u, v, u_x, v_x, u_y, v_y, u * u_x + v * u_y, u * v_x + v * v_y)
-
-    def smoothed(first, second):
-        along = []
-        for channel in (first, second):
-            high, low = split(channel)
-            along.append(dot(high, x_high) + (dot(low, x_high) + dot(high, x_low)))
-        high, low = split(jnp.concatenate(along, axis=1))
+        here = jnp.where((lane >= EDGE) & (lane < EDGE + RIM), east_uv[c], ring[c, 0:n_ext, :])
+        ring[c, 0:n_ext, :] = jnp.where((lane >= west_lane) & (lane < west_lane + RIM), west_uv[c], here)
+
+    channels = derived(ring)
+
+    def smoothed(i):
+        sums = [inner_sum[j] + along(channels[j], x_edge) for j in (i, i + 1)]
+        high, low = split(jnp.concatenate(sums, axis=1))
         both = dot(y_high, high) + (dot(y_high, low) + dot(y_low, high))
         return both[:n_rows, :n_cols], both[:n_rows, LANES : LANES + n_cols]
 
     smooth = []
     for i in range(0, 8, 2):
-        smooth += smoothed(channels[i], channels[i + 1])
+        smooth += smoothed(i)
     fine = (
         smooth[6] - (smooth[0] * smooth[2] + smooth[1] * smooth[4]),
         smooth[7] - (smooth[0] * smooth[3] + smooth[1] * smooth[5]),
@@ -302,35 +335,33 @@
     tiles = lax.axis_size("tile")
     halo = ceil_to(RIM, 8)
     assert n_rows == 3 * halo and lax.axis_size("sub") == 2
-    assert RIM <= n_cols <= LANES and n_cols + 2 * RIM <= RING and 3 * RIM <= LANES
+    assert RIM <= n_cols <= LANES and 3 * RIM <= LANES
     n_ext = n_rows + 2 * halo
     f32 = jnp.float32
     return pl.pallas_call(
         kernel,
         out_shape=jax.ShapeDtypeStruct((2, n_rows // POOL, n_cols // POOL), f32),
-        in_specs=[
-            pl.BlockSpec(memory_space=pltpu.SMEM),
-            pl.BlockSpec(memory_space=pltpu.SMEM),
-            pl.BlockSpec(memory_space=pl.ANY),
-            pl.BlockSpec(memory_space=pl.ANY),
-        ],
+        in_specs=[pl.BlockSpec(memory_space=pltpu.HBM)] * 4,
         out_specs=pl.BlockSpec(memory_space=pltpu.VMEM),
         scratch_shapes=[
+            pltpu.SMEM(east_face.shape, jnp.int32),
+            pltpu.SMEM(seam_turn.shape, jnp.int32),
             pltpu.VMEM(velocity.shape, f32),
             pltpu.VMEM(wet_bits.shape, jnp.int32),
-            pltpu.VMEM((2, n_ext, LANES), f32),
+            pltpu.VMEM((2, n_ext + 8, LANES), f32),
             pltpu.VMEM((2, 2 * halo, LANES), f32),
             pltpu.VMEM((tiles + 1, 4 * halo, LANES), f32),
-            pltpu.VMEM((2, n_ext + 8, RING), f32),
+            pltpu.VMEM((2, n_ext + 8, LANES), f32),
+            pltpu.VMEM((8, ceil_to(n_rows + 2 * R, 16), LANES), f32),
             pltpu.VMEM((2, n_rows, LANES), f32),
-            pltpu.SemaphoreType.DMA((2,)),
+            pltpu.SemaphoreType.DMA((4,)),
             pltpu.SemaphoreType.DMA((2,)),
             pltpu.SemaphoreType.DMA((2,)),
             pltpu.SemaphoreType.DMA((3, tiles + 1)),
             pltpu.SemaphoreType.DMA((3, tiles + 1)),
         ],
         compiler_params=pltpu.CompilerParams(
-            collective_id=0, has_side_effects=True, vmem_limit_bytes=32 * 1024 * 1024
+            collective_id=0, has_side_effects=True, vmem_limit_bytes=60 * 1024 * 1024
         ),
     )(east_face, seam_turn, velocity, wet_bits)
 

time: 19.4 us -> 16.3 us (0.84)
  local copies, waits for them, and re-layouts: 3.53 us -> 1.39 us
  Pallas kernels: 15.7 us -> 14.7 us
    unnamed x8 -> x0, local copies, waits for them, and re-layouts: 2.89 us -> none
    pallas_call x1, Pallas kernels: 15.7 us -> 14.7 us  [on_device(): pl.pallas_call(kernel, out_shape=jax.ShapeDtypeStruct((2, n_rows // POOL,...]
    pallas_call x1, local copies, waits for them, and re-layouts: 0.64 us -> 1.39 us  [on_device(): pl.pallas_call(kernel, out_shape=jax.ShapeDtypeStruct((2, n_rows // POOL,...]
where the time goes in v2:
time: 16.3 us; the launch traced here: 16.1 us
  Pallas kernels  14.7 us (90%)
  local copies, waits for them, and re-layouts  1.39 us (9%)
    pallas_call x1, Pallas kernels, on_device(): pl.pallas_call(kernel, out_shape=jax.ShapeDtypeStruct((2, n_rows // POOL,...  14.7 us
    pallas_call x1, local copies, waits for them, and re-layouts, on_device(): pl.pallas_call(kernel, out_shape=jax.ShapeDtypeStruct((2, n_rows // POOL,...  1.39 us

profile of v2, /device:TPU:0, one launch (start us, length us, event | category | flops | bytes accessed | tf_op | source)
XLA Modules:
  0.0 16.1 jit_solution(3700995982209865993)
XLA Ops:
  0.0 14.7 %shard_map.46 = f32[2,30,30]{2,1,0:T(8,128)} custom-call(s32[4]{0:T(128)} %face_hbm.1, s32[4]{0:T(128)} %turn_hbm.1, f32[2,120,120]{2,1,0:T(8,128)} %vel_hbm.1, s32[4,120]{1,0:T(4,128)} %bits_hbm.1), custom_call_target="tpu_custom_call" | custom-call | tf_op jit(solution)/shard_map/pallas_call | solution.py:341
  14.7 1.4 %copy.5 = f32[2,30,30]{2,0,1:T(2,128)} copy(f32[2,30,30]{2,1,0:T(8,128)} %shard_map.46) | data formatting | bytes 14400 | tf_op jit(solution)/shard_map/pallas_call | solution.py:341

commit v3 on v2

--- a/solution.py
+++ b/solution.py
@@ -48,7 +48,7 @@
 
 def kernel(
     face_hbm, turn_hbm, vel_hbm, bits_hbm, out_ref,
-    face_ref, turn_ref, vel, bits, ext, strips, seams, ring, inner_sum, pooled,
+    face_ref, turn_ref, vel, bits, ext, strips, seams, ring, inner_field, inner_advect, pooled,
     load_sem, row_send, row_recv, strip_send, strip_recv,
 ):
     tiles, rows = lax.axis_size("tile"), lax.axis_size("row")
@@ -192,26 +192,50 @@
     place = lax.broadcasted_iota(jnp.int32, (LANES, LANES), 0)
     x_out = lax.broadcasted_iota(jnp.int32, (LANES, LANES), 1)
 
-    def x_weights(x_in, keep):
+    def field_weights(distance, keep, axis):
+        weight = gaussian(distance, keep(0))
+        slope = DERIV_SCALE * (gaussian(distance - 1, keep(-1)) - gaussian(distance + 1, keep(1)))
+        return split(jnp.concatenate([weight, slope], axis=axis))
+
+    def x_field_weights(x_in, keep):
+        high, low = field_weights(x_in - x_out, lambda step: keep & (x_out < n_cols), 1)
+        return jnp.concatenate([high, high], axis=0), low
+
+    def x_advect_weights(x_in, keep):
         high, low = split(gaussian(x_in - x_out, keep & (x_out < n_cols)))
         above = jnp.concatenate([high, low], axis=1)
         below = jnp.concatenate([high, jnp.zeros_like(low)], axis=1)
         return jnp.concatenate([above, below], axis=0)
 
-    x_own = x_weights(place, (place >= 1) & (place <= n_cols - 2))
+    x_own_field = x_field_weights(place, place < n_cols)
+    x_own_advect = x_advect_weights(place, (place >= 1) & (place <= n_cols - 2))
     at_east = place < LANES // 2
-    x_edge = x_weights(
-        jnp.where(at_east, place + (n_cols - EDGE), place - (west_lane + RIM)),
-        ((place >= 1) & (place <= RIM)) | ((place > west_lane) & (place <= west_lane + RIM)),
+    x_edge = jnp.where(at_east, place + (n_cols - EDGE), place - (west_lane + RIM))
+    x_edge_field = x_field_weights(
+        x_edge, ((place >= EDGE) & (place <= RIM + 1)) | ((place >= west_lane) & (place < west_lane + RIM))
+    )
+    x_edge_advect = x_advect_weights(
+        x_edge, ((place >= 1) & (place <= RIM)) | ((place > west_lane) & (place <= west_lane + RIM))
     )
     top = halo - R
     span = ceil_to(n_rows + 2 * R, 16)
+    n_ext = n_rows + 2 * halo
+    n_field = ext.shape[1]
     span_out = ceil_to(n_rows, 16)
-    y_out = lax.broadcasted_iota(jnp.int32, (span_out, span), 0)
-    y_in = lax.broadcasted_iota(jnp.int32, (span_out, span), 1) - R
-    y_global = y_in + row * n_rows
-    inside = (y_global >= 0) & (y_global < rows * n_rows) & (y_out < n_rows)
-    y_high, y_low = split(gaussian(y_in - y_out, inside))
+
+    def y_places(length, start):
+        y_out = lax.broadcasted_iota(jnp.int32, (span_out, length), 0)
+        y_in = lax.broadcasted_iota(jnp.int32, (span_out, length), 1) + start
+
+        def keep(step):
+            y_global = y_in + step + row * n_rows
+            return (y_global >= 0) & (y_global < rows * n_rows) & (y_out < n_rows)
+
+        return y_in - y_out, keep
+
+    y_field_high, y_field_low = field_weights(*y_places(n_field, -halo), 0)
+    distance, keep = y_places(span, -R)
+    y_high, y_low = split(gaussian(distance, keep(0)))
 
     west = jnp.int32(0)
     for i in range(tiles):
@@ -237,13 +261,17 @@
         grad_y = DERIV_SCALE * (field[c, top + 1 : top + 1 + span, :] - field[c, top - 1 : top - 1 + span, :])
         return centre, grad_x, grad_y
 
-    def derived(field):
+    def advected(field):
         u, u_x, u_y = derive(field, 0)
         v, v_x, v_y = derive(field, 1)
-        return u, v, u_x, v_x, u_y, v_y, u * u_x + v * u_y, u * v_x + v * v_y
-
-    def along(channel, weights):
-        both = dot(jnp.concatenate(split(channel), axis=1), weights)
+        return u * u_x + v * u_y, u * v_x + v * v_y
+
+    def along_field(value, weights):
+        high, low = split(value)
+        return dot(jnp.concatenate([high, low], axis=1), weights[0]) + dot(high, weights[1])
+
+    def along_advect(value, weights):
+        both = dot(jnp.concatenate(split(value), axis=1), weights)
         return both[:, :LANES] + both[:, LANES:]
 
     @pl.when(has_up)
@@ -254,10 +282,10 @@
     def _():
         row_copy(2, row).wait_recv()
 
-    for i, channel in enumerate(derived(ext)):
-        inner_sum[i] = along(channel, x_own)
-
-    n_ext = n_rows + 2 * halo
+    for c, advect in enumerate(advected(ext)):
+        inner_field[c] = along_field(ext[c], x_own_field)
+        inner_advect[c] = along_advect(advect, x_own_advect)
+
     lane = lax.broadcasted_iota(jnp.int32, (n_ext, LANES), 1)
     for c in range(2):
         own = ext[c, 0:n_ext, :]
@@ -296,20 +324,21 @@
         here = jnp.where((lane >= EDGE) & (lane < EDGE + RIM), east_uv[c], ring[c, 0:n_ext, :])
         ring[c, 0:n_ext, :] = jnp.where((lane >= west_lane) & (lane < west_lane + RIM), west_uv[c], here)
 
-    channels = derived(ring)
-
-    def smoothed(i):
-        sums = [inner_sum[j] + along(channels[j], x_edge) for j in (i, i + 1)]
-        high, low = split(jnp.concatenate(sums, axis=1))
-        both = dot(y_high, high) + (dot(y_high, low) + dot(y_low, high))
-        return both[:n_rows, :n_cols], both[:n_rows, LANES : LANES + n_cols]
+    def smoothed(value, high, low):
+        value_high, value_low = split(value)
+        return dot(high, value_high) + (dot(high, value_low) + dot(low, value_high))
 
     smooth = []
-    for i in range(0, 8, 2):
-        smooth += smoothed(i)
+    for c in range(2):
+        field = inner_field[c] + along_field(ring[c], x_edge_field)
+        both = smoothed(field, y_field_high, y_field_low)
+        smooth.append((both[:span_out, :LANES], both[:span_out, LANES:], both[span_out:, :LANES]))
+    advect = [inner_advect[c] + along_advect(a, x_edge_advect) for c, a in enumerate(advected(ring))]
+    advect = smoothed(jnp.concatenate(advect, axis=1), y_high, y_low)
+    (u, u_x, u_y), (v, v_x, v_y) = smooth
     fine = (
-        smooth[6] - (smooth[0] * smooth[2] + smooth[1] * smooth[4]),
-        smooth[7] - (smooth[0] * smooth[3] + smooth[1] * smooth[5]),
+        advect[:, :LANES] - (u * u_x + v * u_y),
+        advect[:, LANES:] - (u * v_x + v * v_y),
     )
 
     n_out = n_rows // POOL
@@ -320,7 +349,7 @@
     mean = mean.astype(jnp.bfloat16)
     for c in range(2):
         pooled[c] = jnp.zeros((n_rows, LANES), jnp.float32)
-        pooled[c, :, 0:n_cols] = fine[c] * wet
+        pooled[c, :, 0:n_cols] = fine[c][:n_rows, :n_cols] * wet
         total = pooled[c, pl.ds(0, n_out, stride=POOL), :]
         for k in range(1, POOL):
             total = total + pooled[c, pl.ds(k, n_out, stride=POOL), :]
@@ -340,7 +369,7 @@
     f32 = jnp.float32
     return pl.pallas_call(
         kernel,
-        out_shape=jax.ShapeDtypeStruct((2, n_rows // POOL, n_cols // POOL), f32),
+        out_shape=pltpu.VMEM((2, n_rows // POOL, n_cols // POOL), f32),
         in_specs=[pl.BlockSpec(memory_space=pltpu.HBM)] * 4,
         out_specs=pl.BlockSpec(memory_space=pltpu.VMEM),
         scratch_shapes=[
@@ -352,7 +381,8 @@
             pltpu.VMEM((2, 2 * halo, LANES), f32),
             pltpu.VMEM((tiles + 1, 4 * halo, LANES), f32),
             pltpu.VMEM((2, n_ext + 8, LANES), f32),
-            pltpu.VMEM((8, ceil_to(n_rows + 2 * R, 16), LANES), f32),
+            pltpu.VMEM((2, n_ext + 8, 2 * LANES), f32),
+            pltpu.VMEM((2, ceil_to(n_rows + 2 * R, 16), LANES), f32),
             pltpu.VMEM((2, n_rows, LANES), f32),
             pltpu.SemaphoreType.DMA((4,)),
             pltpu.SemaphoreType.DMA((2,)),

time: 16.3 us -> 15.4 us (0.945)
  local copies, waits for them, and re-layouts: 1.39 us -> 0.64 us
    pallas_call x1, local copies, waits for them, and re-layouts: 1.39 us -> 0.64 us  [on_device(): pl.pallas_call(kernel, out_shape=pltpu.VMEM((2, n_rows // POOL, n_cols //...]
where the time goes in v3:
time: 15.4 us; the launch traced here: 15.3 us
  Pallas kernels  14.6 us (95%)
  local copies, waits for them, and re-layouts  0.64 us (4%)
    pallas_call x1, Pallas kernels, on_device(): pl.pallas_call(kernel, out_shape=pltpu.VMEM((2, n_rows // POOL, n_cols //...  14.6 us
    pallas_call x1, local copies, waits for them, and re-layouts, on_device(): pl.pallas_call(kernel, out_shape=pltpu.VMEM((2, n_rows // POOL, n_cols //...  0.64 us

profile of v3, /device:TPU:0, one launch (start us, length us, event | category | flops | bytes accessed | tf_op | source)
XLA Modules:
  0.0 15.3 jit_solution(12547229185362517811)
XLA Ops:
  0.0 14.6 %shard_map.46 = f32[2,30,30]{2,1,0:T(8,128)S(1)} custom-call(s32[4]{0:T(128)} %face_hbm.1, s32[4]{0:T(128)} %turn_hbm.1, f32[2,120,120]{2,1,0:T(8,128)} %vel_hbm.1, s32[4,120]{1,0:T(4,128)} %bits_hbm.1), custom_call_target="tpu_custom_call" | custom-call | tf_op jit(solution)/shard_map/pallas_call | solution.py:370
  14.6 0.6 %copy.5 = f32[2,30,30]{2,0,1:T(2,128)} copy(f32[2,30,30]{2,1,0:T(8,128)S(1)} %shard_map.46) | data formatting | bytes 14400 | tf_op jit(solution)/shard_map/pallas_call | solution.py:370

commit v4 on v3

--- a/solution.py
+++ b/solution.py
@@ -48,13 +48,17 @@
 
 def kernel(
     face_hbm, turn_hbm, vel_hbm, bits_hbm, out_ref,
-    face_ref, turn_ref, vel, bits, ext, strips, seams, ring, inner_field, inner_advect, pooled,
-    load_sem, row_send, row_recv, strip_send, strip_recv,
+    face_ref, turn_ref, vel, bits, ext, strips, pieces, picked, seam, beside,
+    ring, inner_field, inner_advect, pooled,
+    load_sem, row_send, row_recv, beside_send, beside_recv,
+    piece_send, piece_recv, seam_send, seam_recv, rim_send, rim_recv,
 ):
     tiles, rows = lax.axis_size("tile"), lax.axis_size("row")
     grp, tile, row, sub = (lax.axis_index(a) for a in ("grp", "tile", "row", "sub"))
     n_rows, n_cols = vel.shape[1], vel.shape[2]
     halo = ceil_to(RIM, 8)
+    piece = pieces.shape[1]
+    part_rows = tiles // 2 * piece
     has_up, has_down = row > 0, row < rows - 1
     other = 1 - sub
 
@@ -75,22 +79,24 @@
     for k in range(tiles):
         t = lax.rem(tile + k, tiles)
         greet(t, row, other)
+        if k:
+            greet(t, row, sub)
 
         @pl.when(has_up)
         def _():
-            greet(t, row - 1, other)
+            greet(t, row - 1, sub)
 
         @pl.when(has_down)
         def _():
-            greet(t, row + 1, other)
+            greet(t, row + 1, sub)
 
     @pl.when(has_up)
     def _():
-        greet(tile, row - 1, sub)
+        greet(tile, row - 1, other)
 
     @pl.when(has_down)
     def _():
-        greet(tile, row + 1, sub)
+        greet(tile, row + 1, other)
 
     for load in loads:
         load.wait()
@@ -127,32 +133,67 @@
     west_cols, east_cols = pack(0), pack(n_cols - RIM)
     at_west = sub == 0
     for i in range(2):
-        at = slice(i * halo, (i + 1) * halo)
+        at = slice(i * part_rows, i * part_rows + halo)
         strips[0, at, :] = jnp.where(at_west, west_cols[i], east_cols[i])
         strips[1, at, :] = jnp.where(at_west, east_cols[i], west_cols[i])
 
     @pl.when(jnp.logical_not(has_up))
     def _():
         ext[:, 0:halo, :] = jnp.zeros((2, halo, LANES), jnp.float32)
-        seams[:, 0:halo, :] = jnp.zeros((tiles + 1, halo, LANES), jnp.float32)
+        seam[0:halo, :] = jnp.zeros((halo, LANES), jnp.float32)
+        beside[0:halo, :] = jnp.zeros((halo, LANES), jnp.float32)
 
     @pl.when(jnp.logical_not(has_down))
     def _():
         ext[:, halo + n_rows : n_rows + 2 * halo, :] = jnp.zeros((2, halo, LANES), jnp.float32)
-        seams[:, 3 * halo :, :] = jnp.zeros((tiles + 1, halo, LANES), jnp.float32)
+        seam[3 * part_rows : 3 * part_rows + halo, :] = jnp.zeros((halo, LANES), jnp.float32)
+        beside[3 * part_rows : 3 * part_rows + halo, :] = jnp.zeros((halo, LANES), jnp.float32)
 
     n_beside = has_up.astype(jnp.int32) + has_down.astype(jnp.int32)
-    pl.semaphore_wait(barrier, tiles + n_beside * (tiles + 1))
-
-    def strip_copy(which, slot, part, k, t, r):
-        source = ((0, 2 * halo), (halo, halo), (0, halo))[part]
-        target = (halo, 0, 3 * halo)[part]
+    pl.semaphore_wait(barrier, 2 * tiles - 1 + n_beside * (tiles + 1))
+
+    def piece_rows(group, q):
+        return pl.ds(pl.multiple_of(group * part_rows + q // 2 * piece, 8), piece)
+
+    def piece_copy(slot, k, q):
         return pltpu.make_async_remote_copy(
-            src_ref=strips.at[which, pl.ds(*source)],
-            dst_ref=seams.at[slot, pl.ds(target, source[1])],
-            send_sem=strip_send.at[part, k],
-            recv_sem=strip_recv.at[part, slot],
-            device_id=(grp, t, r, other),
+            src_ref=strips.at[0, piece_rows(lax.rem(q, 2), q)],
+            dst_ref=pieces.at[slot],
+            send_sem=piece_send.at[k],
+            recv_sem=piece_recv.at[slot],
+            device_id=(grp, q, row, other),
+            device_id_type=MESH,
+        )
+
+    def seam_copy(q, k, t):
+        return pltpu.make_async_remote_copy(
+            src_ref=picked.at[k],
+            dst_ref=seam.at[piece_rows(1 + lax.rem(q, 2), q)],
+            send_sem=seam_send.at[k],
+            recv_sem=seam_recv.at[q],
+            device_id=(grp, t, row, sub),
+            device_id_type=MESH,
+        )
+
+    def rim_copy(q, group, k, t, r):
+        return pltpu.make_async_remote_copy(
+            src_ref=picked.at[k],
+            dst_ref=seam.at[piece_rows(group, q)],
+            send_sem=rim_send.at[k],
+            recv_sem=rim_recv.at[q],
+            device_id=(grp, t, r, sub),
+            device_id_type=MESH,
+        )
+
+    def beside_copy(part, r):
+        source = ((0, 2 * part_rows), (part_rows, halo), (0, halo))[part]
+        target = (part_rows, 0, 3 * part_rows)[part]
+        return pltpu.make_async_remote_copy(
+            src_ref=strips.at[1, pl.ds(*source)],
+            dst_ref=beside.at[pl.ds(target, source[1])],
+            send_sem=beside_send.at[part],
+            recv_sem=beside_recv.at[part],
+            device_id=(grp, tile, r, other),
             device_id_type=MESH,
         )
 
@@ -168,25 +209,37 @@
             device_id_type=MESH,
         )
 
-    def sends(act, part, r):
+    def first_sends(act):
         for k in reversed(range(tiles)):
-            act(strip_copy(0, tile, part, k, lax.rem(tile + k, tiles), r))
-        act(strip_copy(1, tiles, part, tiles, tile, r))
-        if part:
-            act(row_copy(part, r))
-
-    def all_sends(act):
-        sends(act, 0, row)
+            act(piece_copy(tile, k, lax.rem(tile + k, tiles)))
 
         @pl.when(has_down)
         def _():
-            sends(act, 1, row + 1)
+            act(row_copy(1, row + 1))
+            act(beside_copy(1, row + 1))
 
         @pl.when(has_up)
         def _():
-            sends(act, 2, row - 1)
-
-    all_sends(lambda copy: copy.start())
+            act(row_copy(2, row - 1))
+            act(beside_copy(2, row - 1))
+
+        act(beside_copy(0, row))
+
+    odd = lax.rem(tile, 2) == 1
+    rim_row = jnp.where(odd, row + 1, row - 1)
+    rim_group = jnp.where(odd, 0, 3)
+    has_rim = (rim_row >= 0) & (rim_row < rows)
+
+    def second_sends(act):
+        for k in reversed(range(1, tiles)):
+            act(seam_copy(tile, k, lax.rem(tile + k, tiles)))
+
+        @pl.when(has_rim)
+        def _():
+            for k in reversed(range(tiles)):
+                act(rim_copy(tile, rim_group, k, lax.rem(tile + k, tiles), rim_row))
+
+    first_sends(lambda copy: copy.start())
 
     west_lane = LANES - EDGE - RIM
     place = lax.broadcasted_iota(jnp.int32, (LANES, LANES), 0)
@@ -237,13 +290,16 @@
     distance, keep = y_places(span, -R)
     y_high, y_low = split(gaussian(distance, keep(0)))
 
-    west = jnp.int32(0)
-    for i in range(tiles):
-        west = jnp.where(face_ref[i] == tile, i, west)
+    def west_of(t):
+        west = jnp.int32(0)
+        for i in range(tiles):
+            west = jnp.where(face_ref[i] == t, i, west)
+        return west
+
+    west = west_of(tile)
     east_turn = turn_ref[tile]
     west_turn = turn_ref[west]
     west_turn = jnp.where(west_turn == 0, 0, 4 - west_turn)
-    beside = jnp.where(at_west, west, face_ref[tile])
     turn = jnp.where(at_west, west_turn, east_turn)
 
     def choose(a, b):
@@ -251,9 +307,13 @@
 
     cosine, sine = choose(0, 2), choose(1, 3)
 
-    def arrived(part):
-        for slot in range(tiles + 1):
-            strip_copy(0, slot, part, 0, tile, row).wait_recv()
+    for slot in range(tiles):
+        piece_copy(slot, 0, tile).wait_recv()
+    for k in range(tiles):
+        t = lax.rem(tile + k, tiles)
+        picked[k] = pieces[jnp.where(at_west, west_of(t), face_ref[t])]
+    second_sends(lambda copy: copy.start())
+    seam[piece_rows(1 + lax.rem(tile, 2), tile), :] = picked[0]
 
     def derive(field, c):
         centre = field[c, top : top + span, :]
@@ -293,26 +353,32 @@
         ring[c, 0:n_ext, :] = jnp.where(lane < EDGE, roll(own, EDGE - n_cols), rest)
         ring[c, n_ext:, :] = jnp.zeros((8, LANES), jnp.float32)
 
-    arrived(0)
+    beside_copy(0, row).wait_recv()
+    for k in range(1, tiles):
+        seam_copy(lax.rem(tile + k, tiles), 0, tile).wait_recv()
 
     @pl.when(has_up)
     def _():
-        arrived(1)
+        beside_copy(1, row).wait_recv()
+        for q in range(1, tiles, 2):
+            rim_copy(q, 0, 0, tile, row).wait_recv()
 
     @pl.when(has_down)
     def _():
-        arrived(2)
+        beside_copy(2, row).wait_recv()
+        for q in range(0, tiles, 2):
+            rim_copy(q, 3, 0, tile, row).wait_recv()
 
     def unpack(packed, shift):
-        a, b, c, d = (packed[i * halo : (i + 1) * halo] for i in range(4))
+        a, b, c, d = (packed[i * part_rows : i * part_rows + halo] for i in range(4))
         places = (((a, 0), (b, 0), (b, 2), (c, 0), (d, 0)), ((a, 1), (b, 1), (c, 2), (c, 1), (d, 1)))
         return [
             jnp.concatenate([roll(v, shift - p * RIM) for v, p in blocks], axis=0) for blocks in places
         ]
 
-    seam, inner = seams[beside], seams[tiles]
-    east_u, east_v = unpack(jnp.where(at_west, inner, seam), EDGE)
-    west_u, west_v = unpack(jnp.where(at_west, seam, inner), west_lane)
+    outer, inner = seam[...], beside[...]
+    east_u, east_v = unpack(jnp.where(at_west, inner, outer), EDGE)
+    west_u, west_v = unpack(jnp.where(at_west, outer, inner), west_lane)
     east_c = jnp.where(at_west, 1.0, cosine).astype(jnp.float32)
     east_s = jnp.where(at_west, 0.0, sine).astype(jnp.float32)
     west_c = jnp.where(at_west, cosine, 1.0).astype(jnp.float32)
@@ -356,16 +422,19 @@
         high, low = split(total)
         out_ref[c] = dot(high, mean) + dot(low, mean)
 
-    all_sends(lambda copy: copy.wait_send())
+    first_sends(lambda copy: copy.wait_send())
+    second_sends(lambda copy: copy.wait_send())
 
 
 def on_device(velocity, wet_bits, east_face, seam_turn):
     _, n_rows, n_cols = velocity.shape
     tiles = lax.axis_size("tile")
     halo = ceil_to(RIM, 8)
-    assert n_rows == 3 * halo and lax.axis_size("sub") == 2
+    assert n_rows == 3 * halo and lax.axis_size("sub") == 2 and tiles % 2 == 0
     assert RIM <= n_cols <= LANES and 3 * RIM <= LANES
     n_ext = n_rows + 2 * halo
+    piece = ceil_to(-(-halo // (tiles // 2)), 8)
+    part_rows = tiles // 2 * piece
     f32 = jnp.float32
     return pl.pallas_call(
         kernel,
@@ -378,8 +447,11 @@
             pltpu.VMEM(velocity.shape, f32),
             pltpu.VMEM(wet_bits.shape, jnp.int32),
             pltpu.VMEM((2, n_ext + 8, LANES), f32),
-            pltpu.VMEM((2, 2 * halo, LANES), f32),
-            pltpu.VMEM((tiles + 1, 4 * halo, LANES), f32),
+            pltpu.VMEM((2, 2 * part_rows, LANES), f32),
+            pltpu.VMEM((tiles, piece, LANES), f32),
+            pltpu.VMEM((tiles, piece, LANES), f32),
+            pltpu.VMEM((4 * part_rows, LANES), f32),
+            pltpu.VMEM((4 * part_rows, LANES), f32),
             pltpu.VMEM((2, n_ext + 8, LANES), f32),
             pltpu.VMEM((2, n_ext + 8, 2 * LANES), f32),
             pltpu.VMEM((2, ceil_to(n_rows + 2 * R, 16), LANES), f32),
@@ -387,9 +459,10 @@
             pltpu.SemaphoreType.DMA((4,)),
             pltpu.SemaphoreType.DMA((2,)),
             pltpu.SemaphoreType.DMA((2,)),
-            pltpu.SemaphoreType.DMA((3, tiles + 1)),
-            pltpu.SemaphoreType.DMA((3, tiles + 1)),
-        ],
+            pltpu.SemaphoreType.DMA((3,)),
+            pltpu.SemaphoreType.DMA((3,)),
+        ]
+        + [pltpu.SemaphoreType.DMA((tiles,))] * 6,
         compiler_params=pltpu.CompilerParams(
             collective_id=0, has_side_effects=True, vmem_limit_bytes=60 * 1024 * 1024
         ),

time: 15.4 us -> 15.7 us (1.019)
  Pallas kernels: 14.6 us -> 14.9 us
    pallas_call x1, Pallas kernels: 14.6 us -> 14.9 us  [on_device(): pl.pallas_call(kernel, out_shape=pltpu.VMEM((2, n_rows // POOL, n_cols //...]
where the time goes in v4:
time: 15.7 us; the launch traced here: 15.5 us
  Pallas kernels  14.9 us (95%)
  local copies, waits for them, and re-layouts  0.64 us (4%)
    pallas_call x1, Pallas kernels, on_device(): pl.pallas_call(kernel, out_shape=pltpu.VMEM((2, n_rows // POOL, n_cols //...  14.9 us
    pallas_call x1, local copies, waits for them, and re-layouts, on_device(): pl.pallas_call(kernel, out_shape=pltpu.VMEM((2, n_rows // POOL, n_cols //...  0.64 us

profile of v4, /device:TPU:0, one launch (start us, length us, event | category | flops | bytes accessed | tf_op | source)
XLA Modules:
  0.0 15.5 jit_solution(7182325491211539301)
XLA Ops:
  0.0 14.9 %shard_map.46 = f32[2,30,30]{2,1,0:T(8,128)S(1)} custom-call(s32[4]{0:T(128)} %face_hbm.1, s32[4]{0:T(128)} %turn_hbm.1, f32[2,120,120]{2,1,0:T(8,128)} %vel_hbm.1, s32[4,120]{1,0:T(4,128)} %bits_hbm.1), custom_call_target="tpu_custom_call" | custom-call | tf_op jit(solution)/shard_map/pallas_call | solution.py:439
  14.9 0.6 %copy.5 = f32[2,30,30]{2,0,1:T(2,128)} copy(f32[2,30,30]{2,1,0:T(8,128)S(1)} %shard_map.46) | data formatting | bytes 14400 | tf_op jit(solution)/shard_map/pallas_call | solution.py:439

commit v5 on v2

v5 whole, which is shorter than its diff:
```python
import functools
import math

import jax
import jax.numpy as jnp
from jax import lax
from jax.experimental import pallas as pl
from jax.experimental.pallas import tpu as pltpu
from jax.sharding import PartitionSpec as P

R = 32
RIM = R + 1
LANES = 128
EDGE = 2
DERIV_SCALE = 8.0
POOL = 4
WORD_ROWS = 30
MESH = pl.DeviceIdType.MESH

WEIGHT_SUM = sum(math.exp(-0.5 * (k / R) ** 2) for k in range(-R, R + 1))


def ceil_to(value, step):
    return -(-value // step) * step


def gaussian(distance, keep):
    d = distance.astype(jnp.float32) * (1.0 / R)
    weight = jnp.exp(-0.5 * d * d) * (1.0 / WEIGHT_SUM)
    return jnp.where(keep & (jnp.abs(distance) <= R), weight, 0.0)


def split(value):
    high = value.astype(jnp.bfloat16)
    low = (value - high.astype(jnp.float32)).astype(jnp.bfloat16)
    return high, low


def dot(a, b):
    return jnp.dot(a, b, preferred_element_type=jnp.float32)


def roll(value, shift, axis=1):
    size = value.shape[axis]
    shift = shift % size
    return value if shift == 0 else pltpu.roll(value, shift, axis)


def kernel(
    face_hbm, turn_hbm, vel_hbm, bits_hbm, out_ref,
    face_ref, turn_ref, vel, bits, ext, strips, passing, seam, beside,
    ring, inner_field, inner_advect, pooled,
    load_sem, row_send, row_recv, beside_send, beside_recv,
    right_send, left_send, across_send, pass_recv, rim_send, rim_recv,
):
    tiles, rows = lax.axis_size("tile"), lax.axis_size("row")
    grp, tile, row, sub = (lax.axis_index(a) for a in ("grp", "tile", "row", "sub"))
    n_rows, n_cols = vel.shape[1], vel.shape[2]
    halo = ceil_to(RIM, 8)
    has_up, has_down = row > 0, row < rows - 1
    has_left, has_right = tile > 0, tile < tiles - 1
    other = 1 - sub

    loads = [
        pltpu.make_async_copy(vel_hbm, vel, load_sem.at[0]),
        pltpu.make_async_copy(bits_hbm, bits, load_sem.at[1]),
        pltpu.make_async_copy(face_hbm, face_ref, load_sem.at[2]),
        pltpu.make_async_copy(turn_hbm, turn_ref, load_sem.at[3]),
    ]
    for load in loads:
        load.start()

    barrier = pltpu.get_barrier_semaphore()

    def greet(t, r, s):
        pl.semaphore_signal(barrier, inc=1, device_id=(grp, t, r, s), device_id_type=MESH)

    greet(tile, row, other)
    for there, t in ((has_left, tile - 1), (has_right, tile + 1)):

        @pl.when(there)
        def _():
            greet(t, row, other)
            greet(t, row, sub)

    for there, r in ((has_up, row - 1), (has_down, row + 1)):

        @pl.when(there)
        def _():
            greet(tile, r, other)
            greet(tile, r, sub)

    west_lane = LANES - EDGE - RIM
    place = lax.broadcasted_iota(jnp.int32, (LANES, LANES), 0)
    x_out = lax.broadcasted_iota(jnp.int32, (LANES, LANES), 1)

    def field_weights(distance, keep, axis):
        weight = gaussian(distance, keep(0))
        slope = DERIV_SCALE * (gaussian(distance - 1, keep(-1)) - gaussian(distance + 1, keep(1)))
        return split(jnp.concatenate([weight, slope], axis=axis))

    def x_field_weights(x_in, keep):
        high, low = field_weights(x_in - x_out, lambda step: keep & (x_out < n_cols), 1)
        return jnp.concatenate([high, high], axis=0), low

    def x_advect_weights(x_in, keep):
        high, low = split(gaussian(x_in - x_out, keep & (x_out < n_cols)))
        above = jnp.concatenate([high, low], axis=1)
        below = jnp.concatenate([high, jnp.zeros_like(low)], axis=1)
        return jnp.concatenate([above, below], axis=0)

    x_own_field = x_field_weights(place, place < n_cols)
    x_own_advect = x_advect_weights(place, (place >= 1) & (place <= n_cols - 2))
    at_east = place < LANES // 2
    x_edge = jnp.where(at_east, place + (n_cols - EDGE), place - (west_lane + RIM))
    x_edge_field = x_field_weights(
        x_edge, ((place >= EDGE) & (place <= RIM + 1)) | ((place >= west_lane) & (place < west_lane + RIM))
    )
    x_edge_advect = x_advect_weights(
        x_edge, ((place >= 1) & (place <= RIM)) | ((place > west_lane) & (place <= west_lane + RIM))
    )
    top = halo - R
    span = ceil_to(n_rows + 2 * R, 16)
    n_ext = n_rows + 2 * halo
    n_field = ext.shape[1]
    span_out = ceil_to(n_rows, 16)

    def y_places(length, start):
        y_out = lax.broadcasted_iota(jnp.int32, (span_out, length), 0)
        y_in = lax.broadcasted_iota(jnp.int32, (span_out, length), 1) + start

        def keep(step):
            y_global = y_in + step + row * n_rows
            return (y_global >= 0) & (y_global < rows * n_rows) & (y_out < n_rows)

        return y_in - y_out, keep

    y_field_high, y_field_low = field_weights(*y_places(n_field, -halo), 0)
    distance, keep = y_places(span, -R)
    y_high, y_low = split(gaussian(distance, keep(0)))

    for load in loads:
        load.wait()

    row_id = lax.broadcasted_iota(jnp.int32, (n_rows, n_cols), 0)
    words = bits[...]
    word = jnp.broadcast_to(words[0:1], (n_rows, n_cols))
    bit = row_id
    for j in range(1, words.shape[0]):
        here = row_id >= j * WORD_ROWS
        word = jnp.where(here, words[j : j + 1], word)
        bit = jnp.where(here, row_id - j * WORD_ROWS, bit)
    wet = (jnp.right_shift(word, bit) & 1).astype(jnp.float32)
    for c in range(2):
        ext[c, halo : halo + n_rows, :] = jnp.zeros((n_rows, LANES), jnp.float32)
        ext[c, halo : halo + n_rows, 0:n_cols] = vel[c] * wet
        ext[c, n_rows + 2 * halo :, :] = jnp.zeros((8, LANES), jnp.float32)

    lane = lax.broadcasted_iota(jnp.int32, (halo, LANES), 1)

    def pack(start):
        def block(c, g, place):
            rows_at = halo + g * halo
            return roll(ext[c, rows_at : rows_at + halo, :], place * RIM - start)

        def join(a, b, c):
            rest = jnp.where(lane < 3 * RIM, c, 0.0)
            return jnp.where(lane < RIM, a, jnp.where(lane < 2 * RIM, b, rest))

        first = join(block(0, 0, 0), block(1, 0, 1), block(0, 1, 2))
        last = join(block(0, 2, 0), block(1, 2, 1), block(1, 1, 2))
        return first, last

    west_cols, east_cols = pack(0), pack(n_cols - RIM)
    at_west = sub == 0
    for i in range(2):
        at = slice(i * halo, i * halo + halo)
        strips[0, at, :] = jnp.where(at_west, west_cols[i], east_cols[i])
        strips[1, at, :] = jnp.where(at_west, east_cols[i], west_cols[i])

    @pl.when(jnp.logical_not(has_up))
    def _():
        ext[:, 0:halo, :] = jnp.zeros((2, halo, LANES), jnp.float32)
        seam[0:halo, :] = jnp.zeros((halo, LANES), jnp.float32)
        beside[0:halo, :] = jnp.zeros((halo, LANES), jnp.float32)

    @pl.when(jnp.logical_not(has_down))
    def _():
        ext[:, halo + n_rows : n_rows + 2 * halo, :] = jnp.zeros((2, halo, LANES), jnp.float32)
        seam[3 * halo : 3 * halo + halo, :] = jnp.zeros((halo, LANES), jnp.float32)
        beside[3 * halo : 3 * halo + halo, :] = jnp.zeros((halo, LANES), jnp.float32)

    n_beside = sum(there.astype(jnp.int32) for there in (has_up, has_down, has_left, has_right))
    pl.semaphore_wait(barrier, 1 + 2 * n_beside)

    def pass_copy(source, slot, chunk, send, t, to):
        at = pl.ds(chunk * halo, halo)
        return pltpu.make_async_remote_copy(
            src_ref=source.at[at],
            dst_ref=passing.at[slot, at],
            send_sem=send,
            recv_sem=pass_recv.at[slot, chunk],
            device_id=(grp, t, row, to),
            device_id_type=MESH,
        )

    def pass_right(source, slot, chunk, to):
        return pass_copy(source, slot, chunk, right_send.at[slot, chunk], tile + 1, to)

    def pass_left(source, slot, chunk, to):
        return pass_copy(source, slot, chunk, left_send.at[slot, chunk], tile - 1, to)

    def rim_copy(part, r):
        source = (2 * halo, halo)[part - 1]
        target = (0, 3 * halo)[part - 1]
        return pltpu.make_async_remote_copy(
            src_ref=seam.at[pl.ds(source, halo)],
            dst_ref=seam.at[pl.ds(target, halo)],
            send_sem=rim_send.at[part - 1],
            recv_sem=rim_recv.at[part - 1],
            device_id=(grp, tile, r, sub),
            device_id_type=MESH,
        )

    def beside_copy(part, r):
        source = ((0, 2 * halo), (halo, halo), (0, halo))[part]
        target = (halo, 0, 3 * halo)[part]
        return pltpu.make_async_remote_copy(
            src_ref=strips.at[1, pl.ds(*source)],
            dst_ref=beside.at[pl.ds(target, source[1])],
            send_sem=beside_send.at[part],
            recv_sem=beside_recv.at[part],
            device_id=(grp, tile, r, other),
            device_id_type=MESH,
        )

    def row_copy(part, r):
        source = (halo + n_rows - halo, halo)[part - 1]
        target = (0, halo + n_rows)[part - 1]
        return pltpu.make_async_remote_copy(
            src_ref=ext.at[:, pl.ds(source, halo)],
            dst_ref=ext.at[:, pl.ds(target, halo)],
            send_sem=row_send.at[part - 1],
            recv_sem=row_recv.at[part - 1],
            device_id=(grp, tile, r, sub),
            device_id_type=MESH,
        )

    def first_sends(act):
        @pl.when(has_left)
        def _():
            for chunk in range(2):
                act(pass_left(strips.at[0], tile, chunk, other))

        @pl.when(has_right)
        def _():
            for chunk in range(2):
                act(pass_right(strips.at[0], tile, chunk, other))

        @pl.when(has_down)
        def _():
            act(row_copy(1, row + 1))
            act(beside_copy(1, row + 1))

        @pl.when(has_up)
        def _():
            act(row_copy(2, row - 1))
            act(beside_copy(2, row - 1))

        act(beside_copy(0, row))
        for chunk in range(2):
            act(pass_copy(strips.at[0], tile, chunk, across_send.at[chunk], tile, other))

    def pass_on(step, act):
        for chunk in range(2):
            for slot, there, more, onward in (
                (tile + step, tile + step < tiles, has_left, pass_left),
                (tile - step, tile - step >= 0, has_right, pass_right),
            ):

                @pl.when(there)
                def _():
                    act(slot, chunk, more, onward)

    def receive(slot, chunk, more, onward):
        pass_copy(passing.at[slot], slot, chunk, across_send.at[0], tile, other).wait_recv()

        @pl.when(more)
        def _():
            onward(passing.at[slot], slot, chunk, sub).start()

    def sent(slot, chunk, more, onward):
        @pl.when(more)
        def _():
            onward(passing.at[slot], slot, chunk, sub).wait_send()

    def rim_sends(act):
        @pl.when(has_down)
        def _():
            act(rim_copy(1, row + 1))

        @pl.when(has_up)
        def _():
            act(rim_copy(2, row - 1))

    first_sends(lambda copy: copy.start())

    west = jnp.int32(0)
    for i in range(tiles):
        west = jnp.where(face_ref[i] == tile, i, west)
    across_seam = jnp.where(at_west, west, face_ref[tile])
    east_turn = turn_ref[tile]
    west_turn = turn_ref[west]
    west_turn = jnp.where(west_turn == 0, 0, 4 - west_turn)
    turn = jnp.where(at_west, west_turn, east_turn)

    def choose(a, b):
        return jnp.where(turn == a, 1.0, jnp.where(turn == b, -1.0, 0.0)).astype(jnp.float32)

    cosine, sine = choose(0, 2), choose(1, 3)

    def derive(field, c):
        centre = field[c, top : top + span, :]
        grad_x = DERIV_SCALE * (roll(centre, -1) - roll(centre, 1))
        grad_y = DERIV_SCALE * (field[c, top + 1 : top + 1 + span, :] - field[c, top - 1 : top - 1 + span, :])
        return centre, grad_x, grad_y

    def advected(field):
        u, u_x, u_y = derive(field, 0)
        v, v_x, v_y = derive(field, 1)
        return u * u_x + v * u_y, u * v_x + v * v_y

    def along_field(value, weights):
        high, low = split(value)
        return dot(jnp.concatenate([high, low], axis=1), weights[0]) + dot(high, weights[1])

    def along_advect(value, weights):
        both = dot(jnp.concatenate(split(value), axis=1), weights)
        return both[:, :LANES] + both[:, LANES:]

    @pl.when(has_up)
    def _():
        row_copy(1, row).wait_recv()

    @pl.when(has_down)
    def _():
        row_copy(2, row).wait_recv()

    for c, advect in enumerate(advected(ext)):
        inner_field[c] = along_field(ext[c], x_own_field)
        inner_advect[c] = along_advect(advect, x_own_advect)

    lane = lax.broadcasted_iota(jnp.int32, (n_ext, LANES), 1)
    for c in range(2):
        own = ext[c, 0:n_ext, :]
        rest = jnp.where(lane >= LANES - EDGE, roll(own, -EDGE), 0.0)
        ring[c, 0:n_ext, :] = jnp.where(lane < EDGE, roll(own, EDGE - n_cols), rest)
        ring[c, n_ext:, :] = jnp.zeros((8, LANES), jnp.float32)

    for step in range(1, tiles):
        pass_on(step, receive)
    for chunk in range(2):
        pass_copy(passing.at[tile], tile, chunk, across_send.at[0], tile, other).wait_recv()
    seam[halo : 3 * halo, :] = passing[across_seam]
    rim_sends(lambda copy: copy.start())

    east_c = jnp.where(at_west, 1.0, cosine).astype(jnp.float32)
    east_s = jnp.where(at_west, 0.0, sine).astype(jnp.float32)
    west_c = jnp.where(at_west, cosine, 1.0).astype(jnp.float32)
    west_s = jnp.where(at_west, sine, 0.0).astype(jnp.float32)
    lane = lax.broadcasted_iota(jnp.int32, (halo, LANES), 1)
    in_east = (lane >= EDGE) & (lane < EDGE + RIM)
    in_west = (lane >= west_lane) & (lane < west_lane + RIM)

    def fill(block, u_from, v_from):
        east, west = [], []
        for group, at in (u_from, v_from):
            outer, inner = (held[group * halo : (group + 1) * halo, :] for held in (seam, beside))
            east.append(roll(jnp.where(at_west, inner, outer), EDGE - at * RIM))
            west.append(roll(jnp.where(at_west, outer, inner), west_lane - at * RIM))
        east = (east_c * east[0] - east_s * east[1], east_s * east[0] + east_c * east[1])
        west = (west_c * west[0] - west_s * west[1], west_s * west[0] + west_c * west[1])
        at = slice(block * halo, (block + 1) * halo)
        for c in range(2):
            ring[c, at, :] = jnp.where(in_east, east[c], jnp.where(in_west, west[c], ring[c, at, :]))

    beside_copy(0, row).wait_recv()
    fill(1, (1, 0), (1, 1))
    fill(2, (1, 2), (2, 2))
    fill(3, (2, 0), (2, 1))

    @pl.when(has_up)
    def _():
        beside_copy(1, row).wait_recv()
        rim_copy(1, row).wait_recv()

    @pl.when(has_down)
    def _():
        beside_copy(2, row).wait_recv()
        rim_copy(2, row).wait_recv()

    fill(0, (0, 0), (0, 1))
    fill(4, (3, 0), (3, 1))

    def smoothed(value, high, low):
        value_high, value_low = split(value)
        return dot(high, value_high) + (dot(high, value_low) + dot(low, value_high))

    smooth = []
    for c in range(2):
        field = inner_field[c] + along_field(ring[c], x_edge_field)
        both = smoothed(field, y_field_high, y_field_low)
        smooth.append((both[:span_out, :LANES], both[:span_out, LANES:], both[span_out:, :LANES]))
    advect = [inner_advect[c] + along_advect(a, x_edge_advect) for c, a in enumerate(advected(ring))]
    advect = smoothed(jnp.concatenate(advect, axis=1), y_high, y_low)
    (u, u_x, u_y), (v, v_x, v_y) = smooth
    fine = (
        advect[:, :LANES] - (u * u_x + v * u_y),
        advect[:, LANES:] - (u * v_x + v * v_y),
    )

    n_out = n_rows // POOL
    m_out = n_cols // POOL
    col = lax.broadcasted_iota(jnp.int32, (LANES, m_out), 0)
    block_at = lax.broadcasted_iota(jnp.int32, (LANES, m_out), 1) * POOL
    mean = jnp.where((col >= block_at) & (col < block_at + POOL), 1.0 / POOL**2, 0.0)
    mean = mean.astype(jnp.bfloat16)
    for c in range(2):
        pooled[c] = jnp.zeros((n_rows, LANES), jnp.float32)
        pooled[c, :, 0:n_cols] = fine[c][:n_rows, :n_cols] * wet
        total = pooled[c, pl.ds(0, n_out, stride=POOL), :]
        for k in range(1, POOL):
            total = total + pooled[c, pl.ds(k, n_out, stride=POOL), :]
        high, low = split(total)
        out_ref[c] = dot(high, mean) + dot(low, mean)

    first_sends(lambda copy: copy.wait_send())
    for step in range(1, tiles):
        pass_on(step, sent)
    rim_sends(lambda copy: copy.wait_send())


def on_device(velocity, wet_bits, east_face, seam_turn):
    _, n_rows, n_cols = velocity.shape
    tiles = lax.axis_size("tile")
    halo = ceil_to(RIM, 8)
    assert n_rows == 3 * halo and lax.axis_size("sub") == 2
    assert RIM <= n_cols <= LANES and 3 * RIM <= LANES
    n_ext = n_rows + 2 * halo
    f32 = jnp.float32
    return pl.pallas_call(
        kernel,
        out_shape=pltpu.VMEM((2, n_rows // POOL, n_cols // POOL), f32),
        in_specs=[pl.BlockSpec(memory_space=pltpu.HBM)] * 4,
        out_specs=pl.BlockSpec(memory_space=pltpu.VMEM),
        scratch_shapes=[
            pltpu.SMEM(east_face.shape, jnp.int32),
            pltpu.SMEM(seam_turn.shape, jnp.int32),
            pltpu.VMEM(velocity.shape, f32),
            pltpu.VMEM(wet_bits.shape, jnp.int32),
            pltpu.VMEM((2, n_ext + 8, LANES), f32),
            pltpu.VMEM((2, 2 * halo, LANES), f32),
            pltpu.VMEM((tiles, 2 * halo, LANES), f32),
            pltpu.VMEM((4 * halo, LANES), f32),
            pltpu.VMEM((4 * halo, LANES), f32),
            pltpu.VMEM((2, n_ext + 8, LANES), f32),
            pltpu.VMEM((2, n_ext + 8, 2 * LANES), f32),
            pltpu.VMEM((2, ceil_to(n_rows + 2 * R, 16), LANES), f32),
            pltpu.VMEM((2, n_rows, LANES), f32),
            pltpu.SemaphoreType.DMA((4,)),
            pltpu.SemaphoreType.DMA((2,)),
            pltpu.SemaphoreType.DMA((2,)),
            pltpu.SemaphoreType.DMA((3,)),
            pltpu.SemaphoreType.DMA((3,)),
        ]
        + [pltpu.SemaphoreType.DMA((tiles, 2))] * 2
        + [pltpu.SemaphoreType.DMA((2,)), pltpu.SemaphoreType.DMA((tiles, 2))]
        + [pltpu.SemaphoreType.DMA((2,))] * 2,
        compiler_params=pltpu.CompilerParams(
            collective_id=0, has_side_effects=True, vmem_limit_bytes=60 * 1024 * 1024
        ),
    )(east_face, seam_turn, velocity, wet_bits)


def solution(mesh):
    placed = (
        P(None, ("grp", "row"), ("tile", "sub")),
        P(("grp", "row"), ("tile", "sub")),
        P(),
        P(),
    )
    return jax.shard_map(
        on_device,
        mesh=mesh,
        in_specs=placed,
        out_specs=P(None, ("grp", "row"), ("tile", "sub")),
        check_vma=False,
    )
```

time: 16.3 us -> 18.8 us (1.15)
  Pallas kernels: 14.7 us -> 18 us
  local copies, waits for them, and re-layouts: 1.39 us -> 0.64 us
    pallas_call x1, Pallas kernels: 14.7 us -> 18 us  [on_device(): pl.pallas_call(kernel, out_shape=pltpu.VMEM((2, n_rows // POOL, n_cols //...]
    pallas_call x1, local copies, waits for them, and re-layouts: 1.39 us -> 0.64 us  [on_device(): pl.pallas_call(kernel, out_shape=pltpu.VMEM((2, n_rows // POOL, n_cols //...]
where the time goes in v5:
time: 18.8 us; the launch traced here: 18.6 us
  Pallas kernels  18 us (96%)
  local copies, waits for them, and re-layouts  0.64 us (3%)
    pallas_call x1, Pallas kernels, on_device(): pl.pallas_call(kernel, out_shape=pltpu.VMEM((2, n_rows // POOL, n_cols //...  18 us
    pallas_call x1, local copies, waits for them, and re-layouts, on_device(): pl.pallas_call(kernel, out_shape=pltpu.VMEM((2, n_rows // POOL, n_cols //...  0.64 us

profile of v5, /device:TPU:0, one launch (start us, length us, event | category | flops | bytes accessed | tf_op | source)
XLA Modules:
  0.0 18.6 jit_solution(4014616268176432844)
XLA Ops:
  0.0 18.0 %shard_map.46 = f32[2,30,30]{2,1,0:T(8,128)S(1)} custom-call(s32[4]{0:T(128)} %face_hbm.1, s32[4]{0:T(128)} %turn_hbm.1, f32[2,120,120]{2,1,0:T(8,128)} %vel_hbm.1, s32[4,120]{1,0:T(4,128)} %bits_hbm.1), custom_call_target="tpu_custom_call" | custom-call | tf_op jit(solution)/shard_map/pallas_call | solution.py:451
  18.0 0.6 %copy.5 = f32[2,30,30]{2,0,1:T(2,128)} copy(f32[2,30,30]{2,1,0:T(8,128)S(1)} %shard_map.46) | data formatting | bytes 14400 | tf_op jit(solution)/shard_map/pallas_call | solution.py:451

commit v6 on v5

v6 whole, which is shorter than its diff:
```python
import functools
import math

import jax
import jax.numpy as jnp
from jax import lax
from jax.experimental import pallas as pl
from jax.experimental.pallas import tpu as pltpu
from jax.sharding import PartitionSpec as P

R = 32
RIM = R + 1
LANES = 128
EDGE = 2
DERIV_SCALE = 8.0
POOL = 4
WORD_ROWS = 30
MESH = pl.DeviceIdType.MESH

WEIGHT_SUM = sum(math.exp(-0.5 * (k / R) ** 2) for k in range(-R, R + 1))


def ceil_to(value, step):
    return -(-value // step) * step


def gaussian(distance, keep):
    d = distance.astype(jnp.float32) * (1.0 / R)
    weight = jnp.exp(-0.5 * d * d) * (1.0 / WEIGHT_SUM)
    return jnp.where(keep & (jnp.abs(distance) <= R), weight, 0.0)


def split(value):
    high = value.astype(jnp.bfloat16)
    low = (value - high.astype(jnp.float32)).astype(jnp.bfloat16)
    return high, low


def dot(a, b):
    return jnp.dot(a, b, preferred_element_type=jnp.float32)


def roll(value, shift, axis=1):
    size = value.shape[axis]
    shift = shift % size
    return value if shift == 0 else pltpu.roll(value, shift, axis)


def kernel(
    face_hbm, turn_hbm, vel_hbm, bits_hbm, out_ref,
    face_ref, turn_ref, vel, bits, ext, strip, seams, above, below, beside,
    ring, inner_field, inner_advect, pooled,
    load_sem, row_send, row_recv, beside_send, beside_recv, strip_send, strip_recv,
):
    tiles, rows = lax.axis_size("tile"), lax.axis_size("row")
    grp, tile, row, sub = (lax.axis_index(a) for a in ("grp", "tile", "row", "sub"))
    n_rows, n_cols = vel.shape[1], vel.shape[2]
    halo = ceil_to(RIM, 8)
    has_up, has_down = row > 0, row < rows - 1
    other = 1 - sub

    loads = [
        pltpu.make_async_copy(vel_hbm, vel, load_sem.at[0]),
        pltpu.make_async_copy(bits_hbm, bits, load_sem.at[1]),
        pltpu.make_async_copy(face_hbm, face_ref, load_sem.at[2]),
        pltpu.make_async_copy(turn_hbm, turn_ref, load_sem.at[3]),
    ]
    for load in loads:
        load.start()

    barrier = pltpu.get_barrier_semaphore()

    def greet(t, r, s):
        pl.semaphore_signal(barrier, inc=1, device_id=(grp, t, r, s), device_id_type=MESH)

    for k in range(tiles):
        t = lax.rem(tile + k, tiles)
        greet(t, row, other)
        for there, r in ((has_up, row - 1), (has_down, row + 1)):

            @pl.when(there)
            def _():
                greet(t, r, other)

    for there, r in ((has_up, row - 1), (has_down, row + 1)):

        @pl.when(there)
        def _():
            greet(tile, r, sub)

    west_lane = LANES - EDGE - RIM
    place = lax.broadcasted_iota(jnp.int32, (LANES, LANES), 0)
    x_out = lax.broadcasted_iota(jnp.int32, (LANES, LANES), 1)

    def field_weights(distance, keep, axis):
        weight = gaussian(distance, keep(0))
        slope = DERIV_SCALE * (gaussian(distance - 1, keep(-1)) - gaussian(distance + 1, keep(1)))
        return split(jnp.concatenate([weight, slope], axis=axis))

    def x_field_weights(x_in, keep):
        high, low = field_weights(x_in - x_out, lambda step: keep & (x_out < n_cols), 1)
        return jnp.concatenate([high, high], axis=0), low

    def x_advect_weights(x_in, keep):
        high, low = split(gaussian(x_in - x_out, keep & (x_out < n_cols)))
        above = jnp.concatenate([high, low], axis=1)
        below = jnp.concatenate([high, jnp.zeros_like(low)], axis=1)
        return jnp.concatenate([above, below], axis=0)

    x_own_field = x_field_weights(place, place < n_cols)
    x_own_advect = x_advect_weights(place, (place >= 1) & (place <= n_cols - 2))
    at_east = place < LANES // 2
    x_edge = jnp.where(at_east, place + (n_cols - EDGE), place - (west_lane + RIM))
    x_edge_field = x_field_weights(
        x_edge, ((place >= EDGE) & (place <= RIM + 1)) | ((place >= west_lane) & (place < west_lane + RIM))
    )
    x_edge_advect = x_advect_weights(
        x_edge, ((place >= 1) & (place <= RIM)) | ((place > west_lane) & (place <= west_lane + RIM))
    )
    top = halo - R
    span = ceil_to(n_rows + 2 * R, 16)
    n_ext = n_rows + 2 * halo
    n_field = ext.shape[1]
    span_out = ceil_to(n_rows, 16)

    def y_places(length, start):
        y_out = lax.broadcasted_iota(jnp.int32, (span_out, length), 0)
        y_in = lax.broadcasted_iota(jnp.int32, (span_out, length), 1) + start

        def keep(step):
            y_global = y_in + step + row * n_rows
            return (y_global >= 0) & (y_global < rows * n_rows) & (y_out < n_rows)

        return y_in - y_out, keep

    y_field_high, y_field_low = field_weights(*y_places(n_field, -halo), 0)
    distance, keep = y_places(span, -R)
    y_high, y_low = split(gaussian(distance, keep(0)))

    for load in loads:
        load.wait()

    row_id = lax.broadcasted_iota(jnp.int32, (n_rows, n_cols), 0)
    words = bits[...]
    word = jnp.broadcast_to(words[0:1], (n_rows, n_cols))
    bit = row_id
    for j in range(1, words.shape[0]):
        here = row_id >= j * WORD_ROWS
        word = jnp.where(here, words[j : j + 1], word)
        bit = jnp.where(here, row_id - j * WORD_ROWS, bit)
    wet = (jnp.right_shift(word, bit) & 1).astype(jnp.float32)
    for c in range(2):
        ext[c, halo : halo + n_rows, :] = jnp.zeros((n_rows, LANES), jnp.float32)
        ext[c, halo : halo + n_rows, 0:n_cols] = vel[c] * wet
        ext[c, n_rows + 2 * halo :, :] = jnp.zeros((8, LANES), jnp.float32)

    per_row = LANES // R
    deep = halo // 8
    units = 2 * deep
    group = ceil_to(units + 2, per_row) // per_row
    group_rows = group * 8
    strip_rows = strip.shape[0]
    lane = lax.broadcasted_iota(jnp.int32, (8, LANES), 1)

    def place_of(part, i):
        last = (group - 1, units % per_row * R + i)
        if part == "first":
            return divmod(i, per_row), last
        if part == "last":
            at, unit = divmod(i, per_row)
            return (group + at, unit), (group + last[0], last[1])
        last = (last[0], last[1] + units)
        if i < 2:
            return (i * group + group - 1, units % per_row + 1), last
        at, unit = divmod(i - 2, per_row)
        return (2 * group + at, unit), last

    at_west = sub == 0
    lines = [jnp.zeros((8, LANES), jnp.float32)] * (strip_rows // 8)
    for c in range(2):
        own = ext[c, halo : halo + n_rows, :]
        own = jnp.where(at_west, own, roll(own, RIM - n_cols))
        for p, part in enumerate(("first", "middle", "last")):
            for d in range(deep):
                unit = own[(p * deep + d) * 8 : (p * deep + d + 1) * 8]
                (line, at), (last_line, last) = place_of(part, c * deep + d)
                lines[line] = jnp.where(lane // R == at, roll(unit, at * R), lines[line])
                lines[last_line] = jnp.where(lane == last, roll(unit, last - R), lines[last_line])
    for i, line in enumerate(lines):
        strip[i * 8 : (i + 1) * 8, :] = line

    @pl.when(jnp.logical_not(has_up))
    def _():
        ext[:, 0:halo, :] = jnp.zeros((2, halo, LANES), jnp.float32)
        beside[:, 0:halo, :] = jnp.zeros((2, halo, LANES), jnp.float32)
        above[...] = jnp.zeros((tiles, group_rows, LANES), jnp.float32)

    @pl.when(jnp.logical_not(has_down))
    def _():
        ext[:, halo + n_rows : n_rows + 2 * halo, :] = jnp.zeros((2, halo, LANES), jnp.float32)
        beside[:, halo + n_rows :, :] = jnp.zeros((2, halo, LANES), jnp.float32)
        below[...] = jnp.zeros((tiles, group_rows, LANES), jnp.float32)

    n_beside = has_up.astype(jnp.int32) + has_down.astype(jnp.int32)
    pl.semaphore_wait(barrier, tiles + n_beside * (tiles + 1))

    def strip_copy(part, slot, k, t, r):
        source, size = ((0, strip_rows), (group_rows, group_rows), (0, group_rows))[part]
        return pltpu.make_async_remote_copy(
            src_ref=strip.at[pl.ds(source, size)],
            dst_ref=(seams, above, below)[part].at[slot],
            send_sem=strip_send.at[part, k],
            recv_sem=strip_recv.at[part, slot],
            device_id=(grp, t, r, other),
            device_id_type=MESH,
        )

    def beside_copy(part, r):
        source, size = ((halo, n_rows), (n_rows, halo), (halo, halo))[part]
        target = (halo, 0, halo + n_rows)[part]
        return pltpu.make_async_remote_copy(
            src_ref=ext.at[:, pl.ds(source, size)],
            dst_ref=beside.at[:, pl.ds(target, size)],
            send_sem=beside_send.at[part],
            recv_sem=beside_recv.at[part],
            device_id=(grp, tile, r, other),
            device_id_type=MESH,
        )

    def row_copy(part, r):
        source = (halo + n_rows - halo, halo)[part - 1]
        target = (0, halo + n_rows)[part - 1]
        return pltpu.make_async_remote_copy(
            src_ref=ext.at[:, pl.ds(source, halo)],
            dst_ref=ext.at[:, pl.ds(target, halo)],
            send_sem=row_send.at[part - 1],
            recv_sem=row_recv.at[part - 1],
            device_id=(grp, tile, r, sub),
            device_id_type=MESH,
        )

    def strip_sends(act, part, r):
        for k in reversed(range(tiles)):
            act(strip_copy(part, tile, k, lax.rem(tile + k, tiles), r))

    def all_sends(act):
        strip_sends(act, 0, row)
        act(beside_copy(0, row))
        for part, there, r in ((1, has_down, row + 1), (2, has_up, row - 1)):

            @pl.when(there)
            def _():
                act(row_copy(part, r))
                act(beside_copy(part, r))
                strip_sends(act, part, r)

    all_sends(lambda copy: copy.start())

    west = jnp.int32(0)
    for i in range(tiles):
        west = jnp.where(face_ref[i] == tile, i, west)
    across_seam = jnp.where(at_west, west, face_ref[tile])
    east_turn = turn_ref[tile]
    west_turn = turn_ref[west]
    west_turn = jnp.where(west_turn == 0, 0, 4 - west_turn)
    turn = jnp.where(at_west, west_turn, east_turn)

    def choose(a, b):
        return jnp.where(turn == a, 1.0, jnp.where(turn == b, -1.0, 0.0)).astype(jnp.float32)

    cosine, sine = choose(0, 2), choose(1, 3)

    def derive(field, c, start, length):
        centre = field[c, start : start + length, :]
        grad_x = DERIV_SCALE * (roll(centre, -1) - roll(centre, 1))
        grad_y = DERIV_SCALE * (field[c, start + 1 : start + 1 + length, :] - field[c, start - 1 : start - 1 + length, :])
        return centre, grad_x, grad_y

    def advected(field, start, length):
        u, u_x, u_y = derive(field, 0, start, length)
        v, v_x, v_y = derive(field, 1, start, length)
        return u * u_x + v * u_y, u * v_x + v * v_y

    def along_field(value, weights):
        high, low = split(value)
        return dot(jnp.concatenate([high, low], axis=1), weights[0]) + dot(high, weights[1])

    def along_advect(value, weights):
        both = dot(jnp.concatenate(split(value), axis=1), weights)
        return both[:, :LANES] + both[:, LANES:]

    beside_copy(0, row).wait_recv()
    for part, there in ((1, has_up), (2, has_down)):

        @pl.when(there)
        def _():
            row_copy(part, row).wait_recv()
            beside_copy(part, row).wait_recv()

    for c, advect in enumerate(advected(ext, top, span)):
        inner_field[c] = along_field(ext[c], x_own_field)
        inner_advect[c] = along_advect(advect, x_own_advect)

    lane = lax.broadcasted_iota(jnp.int32, (n_ext, LANES), 1)
    inner_at = jnp.where(at_west, EDGE, west_lane)
    in_inner = (lane >= inner_at) & (lane < inner_at + RIM)
    for c in range(2):
        own, inner = ext[c, 0:n_ext, :], beside[c]
        inner = jnp.where(at_west, roll(inner, EDGE), roll(inner, west_lane + RIM - n_cols))
        rest = jnp.where(lane >= LANES - EDGE, roll(own, -EDGE), jnp.where(in_inner, inner, 0.0))
        ring[c, 0:n_ext, :] = jnp.where(lane < EDGE, roll(own, EDGE - n_cols), rest)
        ring[c, n_ext:, :] = jnp.zeros((8, LANES), jnp.float32)

    outer_at = jnp.where(at_west, west_lane, EDGE)
    lane = lax.broadcasted_iota(jnp.int32, (8, LANES), 1)
    in_unit = lane < outer_at + R
    in_outer = (lane >= outer_at) & (lane < outer_at + RIM)

    def lines_of(strips):
        held = strips[across_seam]
        held = jnp.where(at_west, roll(held, west_lane), roll(held, EDGE))
        return [held[i * 8 : (i + 1) * 8] for i in range(held.shape[0] // 8)]

    def fill(lines, part, block):
        for d in range(deep):
            uv = []
            for c in range(2):
                (line, unit), (last_line, last) = place_of(part, c * deep + d)
                uv.append(jnp.where(in_unit, roll(lines[line], -unit * R), roll(lines[last_line], R - last)))
            turned = (cosine * uv[0] - sine * uv[1], sine * uv[0] + cosine * uv[1])
            at = slice((block * deep + d) * 8, (block * deep + d + 1) * 8)
            for c in range(2):
                ring[c, at, :] = jnp.where(in_outer, turned[c], ring[c, at, :])

    def add_field(start, length):
        for c in range(2):
            inner_field[c, start : start + length, :] += along_field(ring[c, start : start + length, :], x_edge_field)

    def add_advect(start, length):
        for c, advect in enumerate(advected(ring, start, length)):
            inner_advect[c, start - top : start - top + length, :] += along_advect(advect, x_edge_advect)

    for slot in range(tiles):
        strip_copy(0, slot, 0, tile, row).wait_recv()
    lines = lines_of(seams)
    fill(lines, "first", 1)
    fill(lines, "middle", 2)
    fill(lines, "last", 3)
    add_field(halo, n_rows)
    add_advect(halo + 8, n_rows - 16)

    for part, there in ((1, has_up), (2, has_down)):

        @pl.when(there)
        def _():
            for slot in range(tiles):
                strip_copy(part, slot, 0, tile, row).wait_recv()

    fill([None] * group + lines_of(above), "last", 0)
    fill(lines_of(below), "first", 4)
    add_field(0, halo)
    add_field(halo + n_rows, n_field - halo - n_rows)
    add_advect(top, halo + 8 - top)
    add_advect(halo + n_rows - 8, top + span - (halo + n_rows - 8))

    def smoothed(value, high, low):
        value_high, value_low = split(value)
        return dot(high, value_high) + (dot(high, value_low) + dot(low, value_high))

    smooth = []
    for c in range(2):
        both = smoothed(inner_field[c], y_field_high, y_field_low)
        smooth.append((both[:span_out, :LANES], both[:span_out, LANES:], both[span_out:, :LANES]))
    advect = smoothed(jnp.concatenate([inner_advect[0], inner_advect[1]], axis=1), y_high, y_low)
    (u, u_x, u_y), (v, v_x, v_y) = smooth
    fine = (
        advect[:, :LANES] - (u * u_x + v * u_y),
        advect[:, LANES:] - (u * v_x + v * v_y),
    )

    n_out = n_rows // POOL
    m_out = n_cols // POOL
    col = lax.broadcasted_iota(jnp.int32, (LANES, m_out), 0)
    block_at = lax.broadcasted_iota(jnp.int32, (LANES, m_out), 1) * POOL
    mean = jnp.where((col >= block_at) & (col < block_at + POOL), 1.0 / POOL**2, 0.0)
    mean = mean.astype(jnp.bfloat16)
    for c in range(2):
        pooled[c] = jnp.zeros((n_rows, LANES), jnp.float32)
        pooled[c, :, 0:n_cols] = fine[c][:n_rows, :n_cols] * wet
        total = pooled[c, pl.ds(0, n_out, stride=POOL), :]
        for k in range(1, POOL):
            total = total + pooled[c, pl.ds(k, n_out, stride=POOL), :]
        high, low = split(total)
        out_ref[c] = dot(high, mean) + dot(low, mean)

    all_sends(lambda copy: copy.wait_send())


def on_device(velocity, wet_bits, east_face, seam_turn):
    _, n_rows, n_cols = velocity.shape
    tiles = lax.axis_size("tile")
    halo = ceil_to(RIM, 8)
    assert n_rows == 3 * halo and lax.axis_size("sub") == 2
    assert 2 * RIM <= n_cols <= LANES and LANES % R == 0
    per_row, units = LANES // R, 2 * halo // 8
    group_rows = ceil_to(units + 2, per_row) // per_row * 8
    strip_rows = 2 * group_rows + ceil_to(units - 2, per_row) // per_row * 8
    assert units % per_row < per_row - 1 and 2 * units <= R
    n_ext = n_rows + 2 * halo
    f32 = jnp.float32
    return pl.pallas_call(
        kernel,
        out_shape=pltpu.VMEM((2, n_rows // POOL, n_cols // POOL), f32),
        in_specs=[pl.BlockSpec(memory_space=pltpu.HBM)] * 4,
        out_specs=pl.BlockSpec(memory_space=pltpu.VMEM),
        scratch_shapes=[
            pltpu.SMEM(east_face.shape, jnp.int32),
            pltpu.SMEM(seam_turn.shape, jnp.int32),
            pltpu.VMEM(velocity.shape, f32),
            pltpu.VMEM(wet_bits.shape, jnp.int32),
            pltpu.VMEM((2, n_ext + 8, LANES), f32),
            pltpu.VMEM((strip_rows, LANES), f32),
            pltpu.VMEM((tiles, strip_rows, LANES), f32),
            pltpu.VMEM((tiles, group_rows, LANES), f32),
            pltpu.VMEM((tiles, group_rows, LANES), f32),
            pltpu.VMEM((2, n_ext, LANES), f32),
            pltpu.VMEM((2, n_ext + 8, LANES), f32),
            pltpu.VMEM((2, n_ext + 8, 2 * LANES), f32),
            pltpu.VMEM((2, ceil_to(n_rows + 2 * R, 16), LANES), f32),
            pltpu.VMEM((2, n_rows, LANES), f32),
            pltpu.SemaphoreType.DMA((4,)),
            pltpu.SemaphoreType.DMA((2,)),
            pltpu.SemaphoreType.DMA((2,)),
            pltpu.SemaphoreType.DMA((3,)),
            pltpu.SemaphoreType.DMA((3,)),
        ]
        + [pltpu.SemaphoreType.DMA((3, tiles))] * 2,
        compiler_params=pltpu.CompilerParams(
            collective_id=0, has_side_effects=True, vmem_limit_bytes=60 * 1024 * 1024
        ),
    )(east_face, seam_turn, velocity, wet_bits)


def solution(mesh):
    placed = (
        P(None, ("grp", "row"), ("tile", "sub")),
        P(("grp", "row"), ("tile", "sub")),
        P(),
        P(),
    )
    return jax.shard_map(
        on_device,
        mesh=mesh,
        in_specs=placed,
        out_specs=P(None, ("grp", "row"), ("tile", "sub")),
        check_vma=False,
    )
```

time: 18.8 us -> 13.4 us (0.71)
  Pallas kernels: 18 us -> 12.7 us
    pallas_call x1, Pallas kernels: 18 us -> 12.7 us  [on_device(): pl.pallas_call(kernel, out_shape=pltpu.VMEM((2, n_rows // POOL, n_cols //...]
where the time goes in v6:
time: 13.4 us; the launch traced here: 13.3 us
  Pallas kernels  12.7 us (95%)
  local copies, waits for them, and re-layouts  0.64 us (5%)
    pallas_call x1, Pallas kernels, on_device(): pl.pallas_call(kernel, out_shape=pltpu.VMEM((2, n_rows // POOL, n_cols //...  12.7 us
    pallas_call x1, local copies, waits for them, and re-layouts, on_device(): pl.pallas_call(kernel, out_shape=pltpu.VMEM((2, n_rows // POOL, n_cols //...  0.64 us

profile of v6, /device:TPU:0, one launch (start us, length us, event | category | flops | bytes accessed | tf_op | source)
XLA Modules:
  0.0 13.3 jit_solution(15342054213972328934)
XLA Ops:
  0.0 12.7 %shard_map.46 = f32[2,30,30]{2,1,0:T(8,128)S(1)} custom-call(s32[4]{0:T(128)} %face_hbm.1, s32[4]{0:T(128)} %turn_hbm.1, f32[2,120,120]{2,1,0:T(8,128)} %vel_hbm.1, s32[4,120]{1,0:T(4,128)} %bits_hbm.1), custom_call_target="tpu_custom_call" | custom-call | tf_op jit(solution)/shard_map/pallas_call | solution.py:411
  12.7 0.6 %copy.5 = f32[2,30,30]{2,0,1:T(2,128)} copy(f32[2,30,30]{2,1,0:T(8,128)S(1)} %shard_map.46) | data formatting | bytes 14400 | tf_op jit(solution)/shard_map/pallas_call | solution.py:411

commit v7 on v6

--- a/solution.py
+++ b/solution.py
@@ -49,7 +49,7 @@
 def kernel(
     face_hbm, turn_hbm, vel_hbm, bits_hbm, out_ref,
     face_ref, turn_ref, vel, bits, ext, strip, seams, above, below, beside,
-    ring, inner_field, inner_advect, pooled,
+    ring, field_sum, advect_sum, pooled,
     load_sem, row_send, row_recv, beside_send, beside_recv, strip_send, strip_recv,
 ):
     tiles, rows = lax.axis_size("tile"), lax.axis_size("row")
@@ -59,6 +59,26 @@
     has_up, has_down = row > 0, row < rows - 1
     other = 1 - sub
 
+    barrier = pltpu.get_barrier_semaphore()
+
+    def greet(t, r, s):
+        pl.semaphore_signal(barrier, inc=1, device_id=(grp, t, r, s), device_id_type=MESH)
+
+    for k in range(tiles):
+        t = lax.rem(tile + k, tiles)
+        greet(t, row, other)
+        for there, r in ((has_up, row - 1), (has_down, row + 1)):
+
+            @pl.when(there)
+            def _():
+                greet(t, r, other)
+
+    for there, r in ((has_up, row - 1), (has_down, row + 1)):
+
+        @pl.when(there)
+        def _():
+            greet(tile, r, sub)
+
     loads = [
         pltpu.make_async_copy(vel_hbm, vel, load_sem.at[0]),
         pltpu.make_async_copy(bits_hbm, bits, load_sem.at[1]),
@@ -68,26 +88,6 @@
     for load in loads:
         load.start()
 
-    barrier = pltpu.get_barrier_semaphore()
-
-    def greet(t, r, s):
-        pl.semaphore_signal(barrier, inc=1, device_id=(grp, t, r, s), device_id_type=MESH)
-
-    for k in range(tiles):
-        t = lax.rem(tile + k, tiles)
-        greet(t, row, other)
-        for there, r in ((has_up, row - 1), (has_down, row + 1)):
-
-            @pl.when(there)
-            def _():
-                greet(t, r, other)
-
-    for there, r in ((has_up, row - 1), (has_down, row + 1)):
-
-        @pl.when(there)
-        def _():
-            greet(tile, r, sub)
-
     west_lane = LANES - EDGE - RIM
     place = lax.broadcasted_iota(jnp.int32, (LANES, LANES), 0)
     x_out = lax.broadcasted_iota(jnp.int32, (LANES, LANES), 1)
@@ -122,20 +122,6 @@
     n_ext = n_rows + 2 * halo
     n_field = ext.shape[1]
     span_out = ceil_to(n_rows, 16)
-
-    def y_places(length, start):
-        y_out = lax.broadcasted_iota(jnp.int32, (span_out, length), 0)
-        y_in = lax.broadcasted_iota(jnp.int32, (span_out, length), 1) + start
-
-        def keep(step):
-            y_global = y_in + step + row * n_rows
-            return (y_global >= 0) & (y_global < rows * n_rows) & (y_out < n_rows)
-
-        return y_in - y_out, keep
-
-    y_field_high, y_field_low = field_weights(*y_places(n_field, -halo), 0)
-    distance, keep = y_places(span, -R)
-    y_high, y_low = split(gaussian(distance, keep(0)))
 
     for load in loads:
         load.wait()
@@ -243,7 +229,7 @@
         for k in reversed(range(tiles)):
             act(strip_copy(part, tile, k, lax.rem(tile + k, tiles), r))
 
-    def all_sends(act):
+    def first_sends(act):
         strip_sends(act, 0, row)
         act(beside_copy(0, row))
         for part, there, r in ((1, has_down, row + 1), (2, has_up, row - 1)):
@@ -252,9 +238,42 @@
             def _():
                 act(row_copy(part, r))
                 act(beside_copy(part, r))
+
+    def rim_sends(act):
+        for part, there, r in ((1, has_down, row + 1), (2, has_up, row - 1)):
+
+            @pl.when(there)
+            def _():
                 strip_sends(act, part, r)
 
-    all_sends(lambda copy: copy.start())
+    first_sends(lambda copy: copy.start())
+    rim_sends(lambda copy: copy.start())
+
+    def y_places(length, place):
+        y_out = lax.broadcasted_iota(jnp.int32, (span_out, length), 0)
+        y_in = place(lax.broadcasted_iota(jnp.int32, (span_out, length), 1))
+
+        def keep(step):
+            y_global = y_in + step + row * n_rows
+            return (y_global >= 0) & (y_global < rows * n_rows) & (y_out < n_rows)
+
+        return y_in - y_out, keep
+
+    def y_field_weights(length, place):
+        return field_weights(*y_places(length, place), 0)
+
+    def y_advect_weights(length, place):
+        distance, keep = y_places(length, place)
+        return split(gaussian(distance, keep(0)))
+
+    y_all_field = y_field_weights(n_field, lambda k: k - halo)
+    y_all_advect = y_advect_weights(span, lambda k: k - R)
+    y_own_field = y_field_weights(n_rows, lambda k: k)
+    y_own_advect = y_advect_weights(n_rows - 16, lambda k: k + 8)
+    y_rim_field = y_field_weights(n_field - n_rows, lambda k: jnp.where(k < halo, k - halo, k - halo + n_rows))
+    y_rim_advect = y_advect_weights(
+        span - n_rows + 16, lambda k: jnp.where(k < R + 8, k - R, k - R + n_rows - 16)
+    )
 
     west = jnp.int32(0)
     for i in range(tiles):
@@ -297,9 +316,21 @@
             row_copy(part, row).wait_recv()
             beside_copy(part, row).wait_recv()
 
-    for c, advect in enumerate(advected(ext, top, span)):
-        inner_field[c] = along_field(ext[c], x_own_field)
-        inner_advect[c] = along_advect(advect, x_own_advect)
+    def smoothed(value, weights):
+        (high, low), (value_high, value_low) = weights, split(value)
+        return dot(high, value_high) + (dot(high, value_low) + dot(low, value_high))
+
+    def smooth_field(parts, x_weights, y_weights):
+        return [smoothed(along_field(part, x_weights), y_weights) for part in parts]
+
+    def smooth_advect(parts, x_weights, y_weights):
+        return smoothed(jnp.concatenate([along_advect(part, x_weights) for part in parts], axis=1), y_weights)
+
+    for c, part in enumerate(smooth_field((ext[0], ext[1]), x_own_field, y_all_field)):
+        field_sum[c] = part
+    advect_sum[...] = smooth_advect(advected(ext, top, span), x_own_advect, y_all_advect)
+    for c in range(2):
+        pooled[c] = jnp.zeros((n_rows, LANES), jnp.float32)
 
     lane = lax.broadcasted_iota(jnp.int32, (n_ext, LANES), 1)
     inner_at = jnp.where(at_west, EDGE, west_lane)
@@ -332,22 +363,17 @@
             for c in range(2):
                 ring[c, at, :] = jnp.where(in_outer, turned[c], ring[c, at, :])
 
-    def add_field(start, length):
-        for c in range(2):
-            inner_field[c, start : start + length, :] += along_field(ring[c, start : start + length, :], x_edge_field)
-
-    def add_advect(start, length):
-        for c, advect in enumerate(advected(ring, start, length)):
-            inner_advect[c, start - top : start - top + length, :] += along_advect(advect, x_edge_advect)
-
     for slot in range(tiles):
         strip_copy(0, slot, 0, tile, row).wait_recv()
     lines = lines_of(seams)
     fill(lines, "first", 1)
     fill(lines, "middle", 2)
     fill(lines, "last", 3)
-    add_field(halo, n_rows)
-    add_advect(halo + 8, n_rows - 16)
+    own_rows = [ring[c, halo : halo + n_rows, :] for c in range(2)]
+    for c, part in enumerate(smooth_field(own_rows, x_edge_field, y_own_field)):
+        field_sum[c] += part
+    advect_sum[...] += smooth_advect(advected(ring, halo + 8, n_rows - 16), x_edge_advect, y_own_advect)
+    first_sends(lambda copy: copy.wait_send())
 
     for part, there in ((1, has_up), (2, has_down)):
 
@@ -358,20 +384,15 @@
 
     fill([None] * group + lines_of(above), "last", 0)
     fill(lines_of(below), "first", 4)
-    add_field(0, halo)
-    add_field(halo + n_rows, n_field - halo - n_rows)
-    add_advect(top, halo + 8 - top)
-    add_advect(halo + n_rows - 8, top + span - (halo + n_rows - 8))
-
-    def smoothed(value, high, low):
-        value_high, value_low = split(value)
-        return dot(high, value_high) + (dot(high, value_low) + dot(low, value_high))
-
+    rim = [jnp.concatenate([ring[c, 0:halo, :], ring[c, halo + n_rows :, :]], axis=0) for c in range(2)]
     smooth = []
-    for c in range(2):
-        both = smoothed(inner_field[c], y_field_high, y_field_low)
+    for c, part in enumerate(smooth_field(rim, x_edge_field, y_rim_field)):
+        both = field_sum[c] + part
         smooth.append((both[:span_out, :LANES], both[:span_out, LANES:], both[span_out:, :LANES]))
-    advect = smoothed(jnp.concatenate([inner_advect[0], inner_advect[1]], axis=1), y_high, y_low)
+    before = advected(ring, top, R + 8)
+    behind = advected(ring, halo + n_rows - 8, span - n_rows + 16 - (R + 8))
+    rim = [jnp.concatenate(pair, axis=0) for pair in zip(before, behind)]
+    advect = advect_sum[...] + smooth_advect(rim, x_edge_advect, y_rim_advect)
     (u, u_x, u_y), (v, v_x, v_y) = smooth
     fine = (
         advect[:, :LANES] - (u * u_x + v * u_y),
@@ -385,7 +406,6 @@
     mean = jnp.where((col >= block_at) & (col < block_at + POOL), 1.0 / POOL**2, 0.0)
     mean = mean.astype(jnp.bfloat16)
     for c in range(2):
-        pooled[c] = jnp.zeros((n_rows, LANES), jnp.float32)
         pooled[c, :, 0:n_cols] = fine[c][:n_rows, :n_cols] * wet
         total = pooled[c, pl.ds(0, n_out, stride=POOL), :]
         for k in range(1, POOL):
@@ -393,7 +413,7 @@
         high, low = split(total)
         out_ref[c] = dot(high, mean) + dot(low, mean)
 
-    all_sends(lambda copy: copy.wait_send())
+    rim_sends(lambda copy: copy.wait_send())
 
 
 def on_device(velocity, wet_bits, east_face, seam_turn):
@@ -425,8 +445,8 @@
             pltpu.VMEM((tiles, group_rows, LANES), f32),
             pltpu.VMEM((2, n_ext, LANES), f32),
             pltpu.VMEM((2, n_ext + 8, LANES), f32),
-            pltpu.VMEM((2, n_ext + 8, 2 * LANES), f32),
-            pltpu.VMEM((2, ceil_to(n_rows + 2 * R, 16), LANES), f32),
+            pltpu.VMEM((2, 2 * ceil_to(n_rows, 16), 2 * LANES), f32),
+            pltpu.VMEM((ceil_to(n_rows, 16), 2 * LANES), f32),
             pltpu.VMEM((2, n_rows, LANES), f32),
             pltpu.SemaphoreType.DMA((4,)),
             pltpu.SemaphoreType.DMA((2,)),

time: 13.4 us -> 13.9 us (1.037)
  Pallas kernels: 12.7 us -> 13.1 us
    pallas_call x1, Pallas kernels: 12.7 us -> 13.1 us  [on_device(): pl.pallas_call(kernel, out_shape=pltpu.VMEM((2, n_rows // POOL, n_cols //...]
where the time goes in v7:
time: 13.9 us; the launch traced here: 13.7 us
  Pallas kernels  13.1 us (94%)
  local copies, waits for them, and re-layouts  0.64 us (5%)
    pallas_call x1, Pallas kernels, on_device(): pl.pallas_call(kernel, out_shape=pltpu.VMEM((2, n_rows // POOL, n_cols //...  13.1 us
    pallas_call x1, local copies, waits for them, and re-layouts, on_device(): pl.pallas_call(kernel, out_shape=pltpu.VMEM((2, n_rows // POOL, n_cols //...  0.64 us

profile of v7, /device:TPU:0, one launch (start us, length us, event | category | flops | bytes accessed | tf_op | source)
XLA Modules:
  0.0 13.7 jit_solution(611055260415075419)
XLA Ops:
  0.0 13.1 %shard_map.46 = f32[2,30,30]{2,1,0:T(8,128)S(1)} custom-call(s32[4]{0:T(128)} %face_hbm.1, s32[4]{0:T(128)} %turn_hbm.1, f32[2,120,120]{2,1,0:T(8,128)} %vel_hbm.1, s32[4,120]{1,0:T(4,128)} %bits_hbm.1), custom_call_target="tpu_custom_call" | custom-call | tf_op jit(solution)/shard_map/pallas_call | solution.py:431
  13.1 0.6 %copy.5 = f32[2,30,30]{2,0,1:T(2,128)} copy(f32[2,30,30]{2,1,0:T(8,128)S(1)} %shard_map.46) | data formatting | bytes 14400 | tf_op jit(solution)/shard_map/pallas_call | solution.py:431

commit v8 on v6

--- a/solution.py
+++ b/solution.py
@@ -73,8 +73,9 @@
     def greet(t, r, s):
         pl.semaphore_signal(barrier, inc=1, device_id=(grp, t, r, s), device_id_type=MESH)
 
-    for k in range(tiles):
-        t = lax.rem(tile + k, tiles)
+    in_left = tile < tiles // 2
+    far_first = [jnp.where(in_left, tiles - 1 - k, k) for k in range(tiles)]
+    for t in far_first:
         greet(t, row, other)
         for there, r in ((has_up, row - 1), (has_down, row + 1)):
 
@@ -240,8 +241,8 @@
         )
 
     def strip_sends(act, part, r):
-        for k in reversed(range(tiles)):
-            act(strip_copy(part, tile, k, lax.rem(tile + k, tiles), r))
+        for k, t in enumerate(far_first):
+            act(strip_copy(part, tile, k, t, r))
 
     def all_sends(act):
         strip_sends(act, 0, row)

time: 13.4 us -> 13.1 us (0.978)
  Pallas kernels: 12.7 us -> 12.3 us
    pallas_call x1, Pallas kernels: 12.7 us -> 12.3 us  [on_device(): pl.pallas_call(kernel, out_shape=pltpu.VMEM((2, n_rows // POOL, n_cols //...]
where the time goes in v8:
time: 13.1 us; the launch traced here: 13 us
  Pallas kernels  12.3 us (94%)
  local copies, waits for them, and re-layouts  0.64 us (5%)
    pallas_call x1, Pallas kernels, on_device(): pl.pallas_call(kernel, out_shape=pltpu.VMEM((2, n_rows // POOL, n_cols //...  12.3 us
    pallas_call x1, local copies, waits for them, and re-layouts, on_device(): pl.pallas_call(kernel, out_shape=pltpu.VMEM((2, n_rows // POOL, n_cols //...  0.64 us

profile of v8, /device:TPU:0, one launch (start us, length us, event | category | flops | bytes accessed | tf_op | source)
XLA Modules:
  0.0 13.0 jit_solution(5033303473344064294)
XLA Ops:
  0.0 12.3 %shard_map.46 = f32[2,30,30]{2,1,0:T(8,128)S(1)} custom-call(s32[4]{0:T(128)} %face_hbm.1, s32[4]{0:T(128)} %turn_hbm.1, f32[2,120,120]{2,1,0:T(8,128)} %vel_hbm.1, s32[4,120]{1,0:T(4,128)} %bits_hbm.1), custom_call_target="tpu_custom_call" | custom-call | tf_op jit(solution)/shard_map/pallas_call | solution.py:412
  12.4 0.6 %copy.5 = f32[2,30,30]{2,0,1:T(2,128)} copy(f32[2,30,30]{2,1,0:T(8,128)S(1)} %shard_map.46) | data formatting | bytes 14400 | tf_op jit(solution)/shard_map/pallas_call | solution.py:412

commit v9 on v7

--- a/solution.py
+++ b/solution.py
@@ -64,8 +64,9 @@
     def greet(t, r, s):
         pl.semaphore_signal(barrier, inc=1, device_id=(grp, t, r, s), device_id_type=MESH)
 
-    for k in range(tiles):
-        t = lax.rem(tile + k, tiles)
+    in_left = tile < tiles // 2
+    far_first = [jnp.where(in_left, tiles - 1 - k, k) for k in range(tiles)]
+    for t in far_first:
         greet(t, row, other)
         for there, r in ((has_up, row - 1), (has_down, row + 1)):
 
@@ -226,8 +227,8 @@
         )
 
     def strip_sends(act, part, r):
-        for k in reversed(range(tiles)):
-            act(strip_copy(part, tile, k, lax.rem(tile + k, tiles), r))
+        for k, t in enumerate(far_first):
+            act(strip_copy(part, tile, k, t, r))
 
     def first_sends(act):
         strip_sends(act, 0, row)

time: 13.9 us -> 13.2 us (0.950)
  Pallas kernels: 13.1 us -> 12.5 us
    pallas_call x1, Pallas kernels: 13.1 us -> 12.5 us  [on_device(): pl.pallas_call(kernel, out_shape=pltpu.VMEM((2, n_rows // POOL, n_cols //...]
where the time goes in v9:
time: 13.2 us; the launch traced here: 13.1 us
  Pallas kernels  12.5 us (95%)
  local copies, waits for them, and re-layouts  0.64 us (5%)
    pallas_call x1, Pallas kernels, on_device(): pl.pallas_call(kernel, out_shape=pltpu.VMEM((2, n_rows // POOL, n_cols //...  12.5 us
    pallas_call x1, local copies, waits for them, and re-layouts, on_device(): pl.pallas_call(kernel, out_shape=pltpu.VMEM((2, n_rows // POOL, n_cols //...  0.64 us

profile of v9, /device:TPU:0, one launch (start us, length us, event | category | flops | bytes accessed | tf_op | source)
XLA Modules:
  0.0 13.1 jit_solution(11374938779078133729)
XLA Ops:
  0.0 12.5 %shard_map.46 = f32[2,30,30]{2,1,0:T(8,128)S(1)} custom-call(s32[4]{0:T(128)} %face_hbm.1, s32[4]{0:T(128)} %turn_hbm.1, f32[2,120,120]{2,1,0:T(8,128)} %vel_hbm.1, s32[4,120]{1,0:T(4,128)} %bits_hbm.1), custom_call_target="tpu_custom_call" | custom-call | tf_op jit(solution)/shard_map/pallas_call | solution.py:432
  12.5 0.6 %copy.5 = f32[2,30,30]{2,0,1:T(2,128)} copy(f32[2,30,30]{2,1,0:T(8,128)S(1)} %shard_map.46) | data formatting | bytes 14400 | tf_op jit(solution)/shard_map/pallas_call | solution.py:432

commit v10 on v9

--- a/solution.py
+++ b/solution.py
@@ -226,12 +226,11 @@
             device_id_type=MESH,
         )
 
-    def strip_sends(act, part, r):
-        for k, t in enumerate(far_first):
-            act(strip_copy(part, tile, k, t, r))
-
-    def first_sends(act):
-        strip_sends(act, 0, row)
+    def strip_sends(act, part, r, ranks):
+        for k in ranks:
+            act(strip_copy(part, tile, k, far_first[k], r))
+
+    def beside_sends(act):
         act(beside_copy(0, row))
         for part, there, r in ((1, has_down, row + 1), (2, has_up, row - 1)):
 
@@ -240,15 +239,20 @@
                 act(row_copy(part, r))
                 act(beside_copy(part, r))
 
-    def rim_sends(act):
+    def rim_sends(act, ranks):
         for part, there, r in ((1, has_down, row + 1), (2, has_up, row - 1)):
 
             @pl.when(there)
             def _():
-                strip_sends(act, part, r)
-
-    first_sends(lambda copy: copy.start())
-    rim_sends(lambda copy: copy.start())
+                strip_sends(act, part, r, ranks)
+
+    far, near = range(tiles // 2), range(tiles // 2, tiles)
+    start, sent = (lambda copy: copy.start()), (lambda copy: copy.wait_send())
+    strip_sends(start, 0, row, far)
+    rim_sends(start, far)
+    beside_sends(start)
+    strip_sends(start, 0, row, near)
+    rim_sends(start, near)
 
     def y_places(length, place):
         y_out = lax.broadcasted_iota(jnp.int32, (span_out, length), 0)
@@ -374,7 +378,8 @@
     for c, part in enumerate(smooth_field(own_rows, x_edge_field, y_own_field)):
         field_sum[c] += part
     advect_sum[...] += smooth_advect(advected(ring, halo + 8, n_rows - 16), x_edge_advect, y_own_advect)
-    first_sends(lambda copy: copy.wait_send())
+    strip_sends(sent, 0, row, range(tiles))
+    beside_sends(sent)
 
     for part, there in ((1, has_up), (2, has_down)):
 
@@ -414,7 +419,7 @@
         high, low = split(total)
         out_ref[c] = dot(high, mean) + dot(low, mean)
 
-    rim_sends(lambda copy: copy.wait_send())
+    rim_sends(sent, range(tiles))
 
 
 def on_device(velocity, wet_bits, east_face, seam_turn):

time: 13.2 us -> 13.2 us (level)
  no operation moved by 1% of the time
where the time goes in v10:
time: 13.2 us; the launch traced here: 13.1 us
  Pallas kernels  12.5 us (95%)
  local copies, waits for them, and re-layouts  0.64 us (5%)
    pallas_call x1, Pallas kernels, on_device(): pl.pallas_call(kernel, out_shape=pltpu.VMEM((2, n_rows // POOL, n_cols //...  12.5 us
    pallas_call x1, local copies, waits for them, and re-layouts, on_device(): pl.pallas_call(kernel, out_shape=pltpu.VMEM((2, n_rows // POOL, n_cols //...  0.64 us

profile of v10, /device:TPU:0, one launch (start us, length us, event | category | flops | bytes accessed | tf_op | source)
XLA Modules:
  0.0 13.1 jit_solution(9540763142766780913)
XLA Ops:
  0.0 12.5 %shard_map.46 = f32[2,30,30]{2,1,0:T(8,128)S(1)} custom-call(s32[4]{0:T(128)} %face_hbm.1, s32[4]{0:T(128)} %turn_hbm.1, f32[2,120,120]{2,1,0:T(8,128)} %vel_hbm.1, s32[4,120]{1,0:T(4,128)} %bits_hbm.1), custom_call_target="tpu_custom_call" | custom-call | tf_op jit(solution)/shard_map/pallas_call | solution.py:437
  12.5 0.6 %copy.5 = f32[2,30,30]{2,0,1:T(2,128)} copy(f32[2,30,30]{2,1,0:T(8,128)S(1)} %shard_map.46) | data formatting | bytes 14400 | tf_op jit(solution)/shard_map/pallas_call | solution.py:437

commit v11 on v10

--- a/solution.py
+++ b/solution.py
@@ -124,7 +124,7 @@
     n_field = ext.shape[1]
     span_out = ceil_to(n_rows, 16)
 
-    for load in loads:
+    for load in loads[:2]:
         load.wait()
 
     row_id = lax.broadcasted_iota(jnp.int32, (n_rows, n_cols), 0)
@@ -279,6 +279,9 @@
     y_rim_advect = y_advect_weights(
         span - n_rows + 16, lambda k: jnp.where(k < R + 8, k - R, k - R + n_rows - 16)
     )
+
+    for load in loads[2:]:
+        load.wait()
 
     west = jnp.int32(0)
     for i in range(tiles):

time: 13.2 us -> 13.2 us (level)
  no operation moved by 1% of the time
where the time goes in v11:
time: 13.2 us; the launch traced here: 13.1 us
  Pallas kernels  12.5 us (95%)
  local copies, waits for them, and re-layouts  0.64 us (5%)
    pallas_call x1, Pallas kernels, on_device(): pl.pallas_call(kernel, out_shape=pltpu.VMEM((2, n_rows // POOL, n_cols //...  12.5 us
    pallas_call x1, local copies, waits for them, and re-layouts, on_device(): pl.pallas_call(kernel, out_shape=pltpu.VMEM((2, n_rows // POOL, n_cols //...  0.64 us

profile of v11, /device:TPU:0, one launch (start us, length us, event | category | flops | bytes accessed | tf_op | source)
XLA Modules:
  0.0 13.1 jit_solution(13392625240343745957)
XLA Ops:
  0.0 12.5 %shard_map.46 = f32[2,30,30]{2,1,0:T(8,128)S(1)} custom-call(s32[4]{0:T(128)} %face_hbm.1, s32[4]{0:T(128)} %turn_hbm.1, f32[2,120,120]{2,1,0:T(8,128)} %vel_hbm.1, s32[4,120]{1,0:T(4,128)} %bits_hbm.1), custom_call_target="tpu_custom_call" | custom-call | tf_op jit(solution)/shard_map/pallas_call | solution.py:440
  12.5 0.6 %copy.5 = f32[2,30,30]{2,0,1:T(2,128)} copy(f32[2,30,30]{2,1,0:T(8,128)S(1)} %shard_map.46) | data formatting | bytes 14400 | tf_op jit(solution)/shard_map/pallas_call | solution.py:440
